TPU v7x, 128 devices: a whole 4x4x4 slice. The times are simulated.
128 devices in a mesh: row: 8 (over y, core), col: 16 (over z, x).
Axes of the slice: x: 4, y: 4, z: 4, core: 2. Of those that a mesh axis runs over, the one named last changes fastest.
Arguments:
- latent: bfloat16 [256, 64, 2048], P(None, 'row', 'col'), may hold values from -6 to 6
- norm_gain: float32 [256], replicated, may hold values from 0.1 to 1.9
- qkv_weight: bfloat16 [768, 256], replicated, may hold values from -0.375 to 0.375
- out_weight: bfloat16 [256, 256], replicated, may hold values from -0.375 to 0.375
- cos_scale: float32 [4], replicated, may hold values from 2 to 12
- grad_output: bfloat16 [256, 64, 2048], P(None, 'row', 'col'), may hold values from -6 to 6
Outputs:
- grad_latent: bfloat16 [256, 64, 2048], P(None, 'row', 'col')
- grad_qkv_weight: float32 [768, 256], replicated
- grad_out_weight: float32 [256, 256], replicated
All inputs are finite; a program needn't handle non-finite values.
Results may differ from a plain program's by a relative error of at most 0.009.
Values may be sent and summed in bfloat16 or wider, within the bound.
A program may use at most 256 MiB of HBM per device.

v0:
```python
import math

import jax
import jax.numpy as jnp
from jax import lax
from jax.sharding import PartitionSpec as P

HEADS = 4
RADIUS = 3


EPS = 1e-06


def with_halo(shard, sides, width):
    for axis, dim in sides:
        size, length = (lax.axis_size(axis), shard.shape[dim])
        up = [(i, (i + 1) % size) for i in range(size - 1)]
        down = [(j, i) for i, j in up]
        last = lax.slice_in_dim(shard, length - width, length, axis=dim)
        first = lax.slice_in_dim(shard, 0, width, axis=dim)
        before = lax.ppermute(last, axis, up)
        after = lax.ppermute(first, axis, down)
        shard = jnp.concatenate([before, shard, after], axis=dim)
    return shard


def shifted(shard, axis, by):
    length = lax.axis_size(axis)
    pairs = [(i, i + by) for i in range(length) if 0 <= i + by < length]
    return lax.ppermute(shard, axis, pairs)


def head_norm(raw):
    inverse = lax.rsqrt(jnp.mean(raw * raw, axis=-3, keepdims=True) + EPS)
    return ((raw * inverse).astype(jnp.bfloat16), inverse)


def norm_back(raw, inverse, grad):
    inner = jnp.mean(grad * raw, axis=-3, keepdims=True)
    return inverse * (grad - raw * inverse * inverse * inner)


def neighbor_pass(queries, key_ext, value_ext, valid_ext, grad_attn, scales):
    head_count, head_width, height, length = queries.shape
    window = 2 * RADIUS + 1
    factor = (scales / head_width)[:, None, None]
    query32 = queries.astype(jnp.float32)
    places = [(a, b) for a in range(window) for b in range(window)]

    def key_at(a, b):
        return key_ext[:, :, a : a + height, b : b + length].astype(jnp.float32)

    def value_at(a, b):
        return value_ext[:, :, a : a + height, b : b + length].astype(jnp.float32)

    def spread(term, a, b):
        return jnp.pad(term, ((0, 0), (0, 0), (a, window - 1 - a), (b, window - 1 - b)))

    exponents = []
    products = []
    for a, b in places:
        logits = factor * jnp.sum(query32 * key_at(a, b), axis=1)
        exponents.append(jnp.exp(logits) * valid_ext[a : a + height, b : b + length])
        products.append(jnp.sum(grad_attn * value_at(a, b), axis=1))
    totals = sum(exponents)
    weights = [item / totals for item in exponents]
    mean_dot = sum((w_item * p_item for w_item, p_item in zip(weights, products)))
    slopes = [factor * w_item * (p_item - mean_dot) for w_item, p_item in zip(weights, products)]
    attn = sum((weights[i][:, None] * value_at(a, b) for i, (a, b) in enumerate(places))).astype(
        jnp.bfloat16
    )
    grad_q = sum((slopes[i][:, None] * key_at(a, b) for i, (a, b) in enumerate(places)))
    grad_k_ext = sum(
        (spread(slopes[i][:, None] * query32, a, b) for i, (a, b) in enumerate(places))
    )
    grad_v_ext = sum(
        (spread(weights[i][:, None] * grad_attn, a, b) for i, (a, b) in enumerate(places))
    )
    return (attn, grad_q, grad_k_ext, grad_v_ext)


def extend(block):
    return with_halo(block, (("row", 1), ("col", 2)), RADIUS)


def pass_columns(block, offset):
    return shifted(block.astype(jnp.bfloat16), "col", offset).astype(block.dtype)


def pass_rows(block, offset):
    return shifted(block.astype(jnp.bfloat16), "row", offset).astype(block.dtype)


def fold_back(extended):
    middle = extended[:, :, RADIUS:-RADIUS]
    middle = middle.at[:, :, -RADIUS:].add(pass_columns(extended[:, :, :RADIUS], -1))
    middle = middle.at[:, :, :RADIUS].add(pass_columns(extended[:, :, -RADIUS:], 1))
    inner = middle[:, RADIUS:-RADIUS]
    inner = inner.at[:, -RADIUS:].add(pass_rows(middle[:, :RADIUS], -1))
    inner = inner.at[:, :RADIUS].add(pass_rows(middle[:, -RADIUS:], 1))
    return inner


def contract_cells(left, right):
    return lax.dot_general(
        left,
        right,
        (((1,), (1,)), ((), ())),
        precision=lax.Precision.HIGHEST,
        preferred_element_type=jnp.float32,
    )


def contract_out(weight, right):
    return lax.dot_general(
        weight.astype(jnp.float32),
        right,
        (((0,), (0,)), ((), ())),
        precision=lax.Precision.HIGHEST,
        preferred_element_type=jnp.float32,
    )


def per_device(latent, norm_gain, qkv_weight, out_weight, cos_scale, grad_output):
    depth, height, length = latent.shape
    head_width = depth // HEADS
    ext_rows = height + 2 * RADIUS
    ext_cols = length + 2 * RADIUS
    latent32 = latent.astype(jnp.float32)
    inverse = lax.rsqrt(jnp.mean(latent32 * latent32, axis=0, keepdims=True) + EPS)
    normed = (latent32 * inverse * norm_gain[:, None, None]).astype(jnp.bfloat16)
    flat = normed.reshape(depth, height * length)
    out_flat = grad_output.reshape(depth, height * length)
    grad_attn = lax.dot_general(
        out_weight, out_flat, (((0,), (0,)), ((), ())), preferred_element_type=jnp.float32
    )
    grad_attn = grad_attn.reshape(HEADS, head_width, height, length)
    row_pos = lax.axis_index("row") * height - RADIUS + jnp.arange(ext_rows, dtype=jnp.int32)
    col_pos = lax.axis_index("col") * length - RADIUS + jnp.arange(ext_cols, dtype=jnp.int32)
    valid_rows = (row_pos >= 0) & (row_pos < height * lax.axis_size("row"))
    valid_cols = (col_pos >= 0) & (col_pos < length * lax.axis_size("col"))
    valid_ext = (valid_rows[:, None] & valid_cols[None, :]).astype(jnp.float32)
    query_raw = jnp.dot(qkv_weight[:depth], flat, preferred_element_type=jnp.float32)
    query_raw = query_raw.reshape(HEADS, head_width, height, length)
    queries, query_inv = head_norm(query_raw)
    pair_raw = jnp.dot(qkv_weight[depth:], flat, preferred_element_type=jnp.float32)
    pair_raw = pair_raw.reshape(2, HEADS, head_width, height, length)
    key_norm, key_inv = head_norm(pair_raw[0])
    values = pair_raw[1].astype(jnp.bfloat16)
    stacked = jnp.stack([key_norm, values]).reshape(2 * depth, height, length)
    stacked_ext = extend(stacked).reshape(2, HEADS, head_width, ext_rows, ext_cols)
    key_ext = stacked_ext[0]
    value_ext = stacked_ext[1]
    attn, grad_q, grad_k_ext, grad_v_ext = neighbor_pass(
        queries, key_ext, value_ext, valid_ext, grad_attn, cos_scale
    )
    attn_flat = attn.reshape(depth, height * length)
    grad_wout = lax.dot_general(
        out_flat, attn_flat, (((1,), (1,)), ((), ())), preferred_element_type=jnp.float32
    )
    grad_qraw = norm_back(query_raw, query_inv, grad_q).reshape(depth, height * length)
    grad_wq = contract_cells(grad_qraw, flat.astype(jnp.float32))
    grad_normed = contract_out(qkv_weight[:depth], grad_qraw)
    both_ext = jnp.stack([grad_k_ext, grad_v_ext]).reshape(2 * depth, ext_rows, ext_cols)
    grad_pair = fold_back(both_ext).reshape(2, HEADS, head_width, height, length)
    grad_kraw = norm_back(pair_raw[0], key_inv, grad_pair[0])
    grad_kv = jnp.stack([grad_kraw, grad_pair[1]]).reshape(2 * depth, height * length)
    grad_wkv = contract_cells(grad_kv, flat.astype(jnp.float32))
    grad_normed = grad_normed + contract_out(qkv_weight[depth:], grad_kv)
    grad_scaled = grad_normed.reshape(depth, height, length) * norm_gain[:, None, None]
    grad_latent = norm_back(latent32, inverse, grad_scaled).astype(jnp.bfloat16)
    local_wqkv = jnp.concatenate([grad_wq, grad_wkv], axis=0)
    summed_wqkv, summed_wout = lax.psum((local_wqkv, grad_wout), ("row", "col"))
    factor = 1.0 / math.sqrt(height * length * lax.axis_size("row") * lax.axis_size("col"))
    return (grad_latent, summed_wqkv * factor, summed_wout * factor)


def solution(mesh):
    return jax.shard_map(
        per_device,
        mesh=mesh,
        in_specs=(P(None, "row", "col"), P(), P(), P(), P(), P(None, "row", "col")),
        out_specs=(P(None, "row", "col"), P(), P()),
        check_vma=False,
    )
```

profile of v0, /device:TPU:1, one launch (start us, length us, event | category | flops | bytes accessed | tf_op | source)
XLA Modules:
  0.0 743.6 jit_solution(11298705166470695197)
XLA Ops:
  14.8 4.6 collective-permute-start
  25.8 4.4 collective-permute-done.1
  30.2 2.7 pad_maximum_fusion.1
  32.9 2.9 fusion.337
  35.8 3.4 copy.138
  39.2 3.4 copy.139
  43.8 4.5 collective-permute-start.2
  52.9 2.8 copy.141
  59.6 3.0 squeeze.21
  62.6 7.4 fusion.345
  70.0 10.8 %fusion.343 = (bf16[4,64,8,128]{1,0,3,2:T(4,128)(2,1)}, bf16[4,64,8,128]{1,0,3,2:T(4,128)(2,1)}, bf16[4,64,8,128]{1,0,3,2:T(4,128)(2,1)}, bf16[4,64,8,128]{1,0,3...) fusion(bf16[4,64,14,134]{1,0,3,2:T(4,128)(2,1)S(1)} %squeeze.21), kind=kLoop, calls=%fused_computation.727 | loop fusion | bytes 19922944 | tf_op jit(solution)/shard_map/slice | solution.py:55
  80.8 10.4 %fusion.344 = (bf16[4,64,8,128]{1,0,3,2:T(4,128)(2,1)}, bf16[4,64,8,128]{1,0,3,2:T(4,128)(2,1)}, bf16[4,64,8,128]{1,0,3,2:T(4,128)(2,1)}, bf16[4,64,8,128]{1,0,3...) fusion(bf16[4,64,14,134]{1,0,3,2:T(4,128)(2,1)S(1)} %squeeze.21), kind=kLoop, calls=%fused_computation.728 | loop fusion | bytes 19922944 | tf_op jit(solution)/shard_map/slice | solution.py:55
  91.1 3.0 squeeze.20
  94.1 7.2 fusion.342
  101.3 10.3 %fusion.341 = (bf16[4,64,8,128]{1,0,3,2:T(4,128)(2,1)}, bf16[4,64,8,128]{1,0,3,2:T(4,128)(2,1)}, bf16[4,64,8,128]{1,0,3,2:T(4,128)(2,1)}, bf16[4,64,8,128]{1,0,3...) fusion(bf16[4,64,14,134]{1,0,3,2:T(4,128)(2,1)S(1)} %squeeze.20), kind=kLoop, calls=%fused_computation.725 | loop fusion | bytes 19922944 | tf_op jit(solution)/shard_map/slice | solution.py:52
  111.7 10.4 %fusion.340 = (bf16[4,64,8,128]{1,0,3,2:T(4,128)(2,1)}, bf16[4,64,8,128]{1,0,3,2:T(4,128)(2,1)}, bf16[4,64,8,128]{1,0,3,2:T(4,128)(2,1)}, bf16[4,64,8,128]{1,0,3...) fusion(bf16[4,64,14,134]{1,0,3,2:T(4,128)(2,1)S(1)} %squeeze.20), kind=kLoop, calls=%fused_computation.724 | loop fusion | bytes 19922944 | tf_op jit(solution)/shard_map/slice | solution.py:52
  122.1 2.4 copy.307
  131.7 2.4 copy.309
  145.9 2.4 copy.261
  182.8 2.4 copy.342
  195.7 2.6 copy.336
  310.2 2.7 copy.290
  328.9 6.9 fusion.61
  336.1 2.8 fusion.88
  339.3 4.0 fusion.207
  343.5 3.1 fusion.206
  346.9 5.4 fusion.87
  352.6 4.4 fusion.208
  357.1 2.4 subtract_multiply_fusion.50
  360.5 4.9 broadcast_multiply_fusion.44
  369.3 5.0 convert_multiply_fusion.12
  374.5 7.7 %convert_multiply_fusion.48 = (f32[4,64,8,128]{3,1,2,0:T(8,128)}, f32[4,64,8,128]{3,1,2,0:T(8,128)}, f32[4,64,8,128]{3,1,2,0:T(8,128)}, f32[4,64,8,128]{3,1,2,0:...) fusion(bf16[4,64,8,128]{3,1,2,0:T(8,128)(2,1)S(1)} %get-tuple-e, ...), kind=kLoop, calls=%fused_computation.48 | loop fusion | flops 4980736 | bytes 19693568 | tf_op jit(solution)/shard_map/mul | solution.py:75
  382.3 16.7 %multiply_reduce_fusion = (f32[4,8,128]{2,1,0:T(8,128)}, f32[4,64,8,128]{3,1,2,0:T(8,128)}) fusion(f32[4,64,8,128]{3,2,1,0:T(8,128)S(1)} %bitcast.102, bf16[4,64,8,128]{3,1,2,0:T(8,128)(2,1)} %copy.301, f32[4,8,128]{2,1,0:T(8,128)} %copy-done.194, bf16[4,64,8,128]{3,1,2,0:T(8,128)(2,1)} %copy.300, f32[4,8,128]{2,1,0:T(8,128)} %copy-done.195, ...), kind=kLoop, calls=%fused_computation.478 | loop fusion | flops 38793216 | bytes 28606464 | tf_op jit(solution)/shard_map/reduce_sum | solution.py:40
  399.2 9.5 %convert_multiply_fusion.30 = (f32[4,64,8,128]{3,1,2,0:T(8,128)}, f32[4,64,8,128]{3,1,2,0:T(8,128)}, f32[4,64,8,128]{3,1,2,0:T(8,128)}, f32[4,64,8,128]{3,1,2,0:...) fusion(bf16[4,64,8,128]{3,1,2,0:T(8,128)(2,1)S(1)} %get-tuple-e, ...), kind=kLoop, calls=%fused_computation.30 | loop fusion | flops 4980736 | bytes 19693568 | tf_op jit(solution)/shard_map/mul | solution.py:75
  409.0 15.2 %fusion.214 = bf16[4,64,8,128]{3,1,2,0:T(8,128)(2,1)} fusion(bf16[4,64,8,128]{3,1,2,0:T(8,128)(2,1)} %copy.350, bf16[4,64,8,128]{3,1,2,0:T(8,128)(2,1)} %copy.349, bf16[4,64,8,128]{3,1,2,0:T(8,128)(2,1)} %copy.348, bf16[4,64,8,128]{3,1,2,0:T(8,128)(2,1)} %copy.347, bf16[4,64,8,128]{3,1,2,0:T(8,128)(2,1)} %copy.346, bf16[4,64,8,128]{3,1,2,0:T(8,128)(2,1)} %copy.345, ...), kind=kLoop, calls=%fused_computation.480 | loop fusion | flops 38535168 | bytes 27017216 | tf_op jit(solution)/shard_map/convert_element_type | solution.py:70
  424.3 6.7 broadcast_multiply_fusion.48
  431.1 9.3 %broadcast_multiply_fusion.45 = (f32[4,64,8,128]{3,1,2,0:T(8,128)}, f32[4,64,8,128]{3,1,2,0:T(8,128)}, f32[4,64,8,128]{3,1,2,0:T(8,128)}, f32[4,64,8,128]{3,1,2,...) fusion(f32[4,64,8,128]{3,1,2,0:T(8,128)S(1)} %get-tuple-element, ...), kind=kLoop, calls=%fused_computation.544 | loop fusion | flops 4718592 | bytes 20217856 | tf_op jit(solution)/shard_map/mul | solution.py:78
  441.8 32.2 %add_bitcast_fusion.1 = f32[1,4,64,14,134]{4,2,3,1,0:T(8,128)S(1)} fusion(f32[4,64,8,128]{3,1,2,0:T(8,128)} %get-tuple-element.421, f32[4,64,8,128]{3,1,2,0:T(8,128)} %get-tuple-element.420, f32[4,64,8,128]{3,1,2,0:T(8,128)} %get-tuple-element.419, f32[4,64,8,128]{3,1,2,0:T(8,128)} %get-tuple-element.418, f32[4,64,8,128]{3,1,2,0:T(8,128)} %get-tuple-element.417, ...), kind=kLoop, calls=%fused_computation.100 | loop fusion | flops 23052288 | bytes 53301248 | tf_op jit(solution)/shard_map/stack | solution.py:165
  474.2 31.4 %add_bitcast_fusion = f32[1,4,64,14,134]{4,2,3,1,0:T(8,128)S(1)} fusion(f32[4,64,8,128]{3,1,2,0:T(8,128)} %get-tuple-element.325, f32[4,64,8,128]{3,1,2,0:T(8,128)} %get-tuple-element.326, f32[4,64,8,128]{3,1,2,0:T(8,128)} %get-tuple-element.327, f32[4,64,8,128]{3,1,2,0:T(8,128)} %get-tuple-element.328, f32[4,64,8,128]{3,1,2,0:T(8,128)} %get-tuple-element.329, ...), kind=kLoop, calls=%fused_computation.99 | loop fusion | flops 23052288 | bytes 53301248 | tf_op jit(solution)/shard_map/stack | solution.py:165
  505.6 4.2 pad_maximum_fusion
  509.8 11.0 %copy.245 = f32[2,4,64,14,134]{2,1,0,4,3:T(4,128)} copy(f32[2,4,64,14,134]{4,2,3,1,0:T(8,128)} %pad_maximum_fusion) | data formatting | bytes 7684096 | tf_op jit(solution)/shard_map/stack | solution.py:165
  520.7 8.5 %reshape.15214 = f32[512,14,134]{0,2,1:T(8,128)} reshape(f32[2,4,64,14,134]{2,1,0,4,3:T(4,128)} %copy.245) | data formatting | bytes 7684096 | tf_op jit(solution)/shard_map/reshape | solution.py:165
  529.3 2.5 convert.12
  537.1 4.0 collective-permute-start.5
  551.2 3.6 collective-permute-start.7
  561.3 2.6 copy.246
  565.2 2.6 copy.248
  578.8 153.9 %all-reduce.101.cloned.1.call-done = (f32[768,256]{1,0:T(8,128)}, f32[256,256]{0,1:T(8,128)}) async-done(((f32[768,256]{1,0:T(8,128)}, f32[256,256]{0,1:T(8,128)}), (f32[768,256]{1,0:T(8,128)}, f32[256,256]{0,1:T(8,128)})) %all-reduce.101.cloned.1.call-update) | async-done | bytes 1048592 | tf_op jit(solution)/shard_map/psum | solution.py:174
  (622 shorter events, 259.7 us)
Async XLA Ops:
  7.2 725.5 %all-reduce.101.cloned.1.call-start = ((), (), s32[]{:S(2)}) async-start(), calls=%async_computation | async-start | bytes 2097152 | tf_op jit(solution)/shard_map/psum | solution.py:174
  9.9 12.9 %copy-start.4 = (bf16[256,8,128]{2,1,0:T(8,128)(2,1)}, bf16[256,8,128]{2,1,0:T(8,128)(2,1)S(1)}, u32[]{:S(2)}) copy-start(bf16[256,8,128]{2,1,0:T(8,128)(2,1)S(1)} %fusion.8) | copy-start | bytes 1572868
  14.8 11.0 %collective-permute-start = (bf16[512,3,128]{2,1,0:T(4,128)(2,1)}, bf16[512,3,128]{2,1,0:T(4,128)(2,1)}, u32[]{:S(2)}, u32[]{:S(2)}) collective-permute-start(bf16[512,3,128]{2,1,0:T(4,128)(2,1)} %get-tuple-element.371), channel_id=1, source_target_pairs={{0,16},{16,32},{32,48},{48,64},{64,80},{80,96},{96,112},{1,17},{17... | collective-permute-start | bytes 1179656 | tf_op jit(solution)/shard_map/ppermute | solution.py:22
  19.4 10.8 %collective-permute-start.1 = (bf16[512,3,128]{2,1,0:T(4,128)(2,1)}, bf16[512,3,128]{2,1,0:T(4,128)(2,1)}, u32[]{:S(2)}, u32[]{:S(2)}) collective-permute-start(bf16[512,3,128]{2,1,0:T(4,128)(2,1)} %get-tuple-element.372), channel_id=1, source_target_pairs={{16,0},{32,16},{48,32},{64,48},{80,64},{96,80},{112,96},{17,1},{33... | collective-permute-start | bytes 1179656 | tf_op jit(solution)/shard_map/ppermute | solution.py:23
  24.8 314.1 %copy-start.191 = (f32[4,8,128]{2,1,0:T(8,128)}, f32[4,8,128]{2,1,0:T(8,128)S(1)}, u32[]{:S(2)}) copy-start(f32[4,8,128]{2,1,0:T(8,128)S(1)} %add_rsqrt_fusion.1) | copy-start | bytes 49156
  35.7 12.5 %copy-start.221 = (f32[4]{0:T(128)S(1)}, f32[4]{0:T(128)}, u32[]{:S(2)}) copy-start(f32[4]{0:T(128)} %param.18) | copy-start | bytes 52
  35.7 13.1 %copy-start.207 = (bf16[256,256]{1,0:T(8,128)(2,1)S(1)}, bf16[256,256]{1,0:T(8,128)(2,1)}, u32[]{:S(2)}) copy-start(bf16[256,256]{1,0:T(8,128)(2,1)} %param.17) | copy-start | bytes 393220
  42.5 13.2 %collective-permute-start.3 = (bf16[512,14,3]{0,1,2:T(8,128)(2,1)}, bf16[512,14,3]{0,1,2:T(8,128)(2,1)S(1)}, u32[]{:S(2)}, u32[]{:S(2)}) collective-permute-start(bf16[512,14,3]{0,1,2:T(8,128)(2,1)} %copy.139), channel_id=1, source_target_pairs={{1,0},{2,1},{3,2},{4,3},{5,4},{6,5},{7,6},{8,7},{9,8},{10,9},{11,1... | collective-permute-start | bytes 129032 | tf_op jit(solution)/shard_map/ppermute | solution.py:23
  43.8 12.0 %collective-permute-start.2 = (bf16[512,14,3]{0,1,2:T(8,128)(2,1)}, bf16[512,14,3]{0,1,2:T(8,128)(2,1)S(1)}, u32[]{:S(2)}, u32[]{:S(2)}) collective-permute-start(bf16[512,14,3]{0,1,2:T(8,128)(2,1)} %copy.138), channel_id=1, source_target_pairs={{0,1},{1,2},{2,3},{3,4},{4,5},{5,6},{6,7},{7,8},{8,9},{9,10},{10,1... | collective-permute-start | bytes 129032 | tf_op jit(solution)/shard_map/ppermute | solution.py:22
  130.4 10.5 %copy-start.114 = (bf16[4,64,8,128]{1,0,3,2:T(4,128)(2,1)S(1)}, bf16[4,64,8,128]{1,0,3,2:T(4,128)(2,1)}, u32[]{:S(2)}) copy-start(bf16[4,64,8,128]{1,0,3,2:T(4,128)(2,1)} %get-tuple-element.318) | copy-start | bytes 1572868
  143.6 11.6 %copy-start.118 = (bf16[4,64,8,128]{1,0,3,2:T(4,128)(2,1)S(1)}, bf16[4,64,8,128]{1,0,3,2:T(4,128)(2,1)}, u32[]{:S(2)}) copy-start(bf16[4,64,8,128]{1,0,3,2:T(4,128)(2,1)} %get-tuple-element.265) | copy-start | bytes 1572868
  145.9 10.6 %copy-start.117 = (bf16[4,64,8,128]{1,0,3,2:T(4,128)(2,1)S(1)}, bf16[4,64,8,128]{1,0,3,2:T(4,128)(2,1)}, u32[]{:S(2)}) copy-start(bf16[4,64,8,128]{1,0,3,2:T(4,128)(2,1)} %get-tuple-element.266) | copy-start | bytes 1572868
  157.9 10.8 %copy-start.112 = (bf16[4,64,8,128]{1,0,3,2:T(4,128)(2,1)S(1)}, bf16[4,64,8,128]{1,0,3,2:T(4,128)(2,1)}, u32[]{:S(2)}) copy-start(bf16[4,64,8,128]{1,0,3,2:T(4,128)(2,1)} %get-tuple-element.272) | copy-start | bytes 1572868
  170.1 11.5 %copy-start.111 = (bf16[4,64,8,128]{1,0,3,2:T(4,128)(2,1)S(1)}, bf16[4,64,8,128]{1,0,3,2:T(4,128)(2,1)}, u32[]{:S(2)}) copy-start(bf16[4,64,8,128]{1,0,3,2:T(4,128)(2,1)} %get-tuple-element.278) | copy-start | bytes 1572868
  182.8 11.5 %copy-start.110 = (bf16[4,64,8,128]{1,0,3,2:T(4,128)(2,1)S(1)}, bf16[4,64,8,128]{1,0,3,2:T(4,128)(2,1)}, u32[]{:S(2)}) copy-start(bf16[4,64,8,128]{1,0,3,2:T(4,128)(2,1)} %get-tuple-element.284) | copy-start | bytes 1572868
  195.7 11.7 %copy-start.109 = (bf16[4,64,8,128]{1,0,3,2:T(4,128)(2,1)S(1)}, bf16[4,64,8,128]{1,0,3,2:T(4,128)(2,1)}, u32[]{:S(2)}) copy-start(bf16[4,64,8,128]{1,0,3,2:T(4,128)(2,1)} %get-tuple-element.290) | copy-start | bytes 1572868
  208.8 11.5 %copy-start.107 = (bf16[4,64,8,128]{1,0,3,2:T(4,128)(2,1)S(1)}, bf16[4,64,8,128]{1,0,3,2:T(4,128)(2,1)}, u32[]{:S(2)}) copy-start(bf16[4,64,8,128]{1,0,3,2:T(4,128)(2,1)} %get-tuple-element.296) | copy-start | bytes 1572868
  221.5 11.5 %copy-start.105 = (bf16[4,64,8,128]{1,0,3,2:T(4,128)(2,1)S(1)}, bf16[4,64,8,128]{1,0,3,2:T(4,128)(2,1)}, u32[]{:S(2)}) copy-start(bf16[4,64,8,128]{1,0,3,2:T(4,128)(2,1)} %get-tuple-element.302) | copy-start | bytes 1572868
  234.3 11.5 %copy-start.103 = (bf16[4,64,8,128]{1,0,3,2:T(4,128)(2,1)S(1)}, bf16[4,64,8,128]{1,0,3,2:T(4,128)(2,1)}, u32[]{:S(2)}) copy-start(bf16[4,64,8,128]{1,0,3,2:T(4,128)(2,1)} %get-tuple-element.308) | copy-start | bytes 1572868
  255.4 11.4 %copy-start.106 = (bf16[4,64,8,128]{1,0,3,2:T(4,128)(2,1)S(1)}, bf16[4,64,8,128]{1,0,3,2:T(4,128)(2,1)}, u32[]{:S(2)}) copy-start(bf16[4,64,8,128]{1,0,3,2:T(4,128)(2,1)} %get-tuple-element.250) | copy-start | bytes 1572868
  268.2 11.5 %copy-start.104 = (bf16[4,64,8,128]{1,0,3,2:T(4,128)(2,1)S(1)}, bf16[4,64,8,128]{1,0,3,2:T(4,128)(2,1)}, u32[]{:S(2)}) copy-start(bf16[4,64,8,128]{1,0,3,2:T(4,128)(2,1)} %get-tuple-element.256) | copy-start | bytes 1572868
  281.0 11.5 %copy-start.102 = (bf16[4,64,8,128]{1,0,3,2:T(4,128)(2,1)S(1)}, bf16[4,64,8,128]{1,0,3,2:T(4,128)(2,1)}, u32[]{:S(2)}) copy-start(bf16[4,64,8,128]{1,0,3,2:T(4,128)(2,1)} %get-tuple-element.224) | copy-start | bytes 1572868
  409.0 15.3 %copy-start.163 = (f32[4,8,128]{2,1,0:T(8,128)S(1)}, f32[4,8,128]{2,1,0:T(8,128)}, u32[]{:S(2)}) copy-start(f32[4,8,128]{2,1,0:T(8,128)} %copy-done.162) | copy-start | bytes 49156
  409.0 15.3 %copy-start.165 = (f32[4,8,128]{2,1,0:T(8,128)S(1)}, f32[4,8,128]{2,1,0:T(8,128)}, u32[]{:S(2)}) copy-start(f32[4,8,128]{2,1,0:T(8,128)} %copy-done.164) | copy-start | bytes 49156
  409.0 15.3 %copy-start.167 = (f32[4,8,128]{2,1,0:T(8,128)S(1)}, f32[4,8,128]{2,1,0:T(8,128)}, u32[]{:S(2)}) copy-start(f32[4,8,128]{2,1,0:T(8,128)} %copy-done.166) | copy-start | bytes 49156
  409.0 15.3 %copy-start.169 = (f32[4,8,128]{2,1,0:T(8,128)S(1)}, f32[4,8,128]{2,1,0:T(8,128)}, u32[]{:S(2)}) copy-start(f32[4,8,128]{2,1,0:T(8,128)} %copy-done.168) | copy-start | bytes 49156
  409.0 15.3 %copy-start.193 = (f32[4,8,128]{2,1,0:T(8,128)S(1)}, f32[4,8,128]{2,1,0:T(8,128)}, u32[]{:S(2)}) copy-start(f32[4,8,128]{2,1,0:T(8,128)} %get-tuple-element.164) | copy-start | bytes 49156
  431.1 10.6 %copy-start.143 = (f32[4,64,8,128]{3,1,2,0:T(8,128)S(1)}, f32[4,64,8,128]{3,1,2,0:T(8,128)}, u32[]{:S(2)}) copy-start(f32[4,64,8,128]{3,1,2,0:T(8,128)} %get-tuple-element.383) | copy-start | bytes 3145732
  441.7 32.3 %copy-start.120 = (f32[4,64,8,128]{3,1,2,0:T(8,128)S(1)}, f32[4,64,8,128]{3,1,2,0:T(8,128)}, u32[]{:S(2)}) copy-start(f32[4,64,8,128]{3,1,2,0:T(8,128)} %get-tuple-element.358) | copy-start | bytes 3145732
  441.7 32.3 %copy-start.121 = (f32[4,64,8,128]{3,1,2,0:T(8,128)S(1)}, f32[4,64,8,128]{3,1,2,0:T(8,128)}, u32[]{:S(2)}) copy-start(f32[4,64,8,128]{3,1,2,0:T(8,128)} %get-tuple-element.359) | copy-start | bytes 3145732
  441.7 32.3 %copy-start.122 = (f32[4,64,8,128]{3,1,2,0:T(8,128)S(1)}, f32[4,64,8,128]{3,1,2,0:T(8,128)}, u32[]{:S(2)}) copy-start(f32[4,64,8,128]{3,1,2,0:T(8,128)} %get-tuple-element.360) | copy-start | bytes 3145732
  441.7 32.3 %copy-start.123 = (f32[4,64,8,128]{3,1,2,0:T(8,128)S(1)}, f32[4,64,8,128]{3,1,2,0:T(8,128)}, u32[]{:S(2)}) copy-start(f32[4,64,8,128]{3,1,2,0:T(8,128)} %get-tuple-element.361) | copy-start | bytes 3145732
  441.7 32.3 %copy-start.124 = (f32[4,64,8,128]{3,1,2,0:T(8,128)S(1)}, f32[4,64,8,128]{3,1,2,0:T(8,128)}, u32[]{:S(2)}) copy-start(f32[4,64,8,128]{3,1,2,0:T(8,128)} %get-tuple-element.362) | copy-start | bytes 3145732
  441.7 32.3 %copy-start.125 = (f32[4,64,8,128]{3,1,2,0:T(8,128)S(1)}, f32[4,64,8,128]{3,1,2,0:T(8,128)}, u32[]{:S(2)}) copy-start(f32[4,64,8,128]{3,1,2,0:T(8,128)} %get-tuple-element.363) | copy-start | bytes 3145732
  441.7 32.3 %copy-start.126 = (f32[4,64,8,128]{3,1,2,0:T(8,128)S(1)}, f32[4,64,8,128]{3,1,2,0:T(8,128)}, u32[]{:S(2)}) copy-start(f32[4,64,8,128]{3,1,2,0:T(8,128)} %get-tuple-element.364) | copy-start | bytes 3145732
  441.8 32.3 %copy-start.127 = (f32[4,64,8,128]{3,1,2,0:T(8,128)S(1)}, f32[4,64,8,128]{3,1,2,0:T(8,128)}, u32[]{:S(2)}) copy-start(f32[4,64,8,128]{3,1,2,0:T(8,128)} %get-tuple-element.365) | copy-start | bytes 3145732
  441.8 32.3 %copy-start.128 = (f32[4,64,8,128]{3,1,2,0:T(8,128)S(1)}, f32[4,64,8,128]{3,1,2,0:T(8,128)}, u32[]{:S(2)}) copy-start(f32[4,64,8,128]{3,1,2,0:T(8,128)} %get-tuple-element.366) | copy-start | bytes 3145732
  441.8 32.3 %copy-start.129 = (f32[4,64,8,128]{3,1,2,0:T(8,128)S(1)}, f32[4,64,8,128]{3,1,2,0:T(8,128)}, u32[]{:S(2)}) copy-start(f32[4,64,8,128]{3,1,2,0:T(8,128)} %get-tuple-element.367) | copy-start | bytes 3145732
  441.8 32.3 %copy-start.130 = (f32[4,64,8,128]{3,1,2,0:T(8,128)S(1)}, f32[4,64,8,128]{3,1,2,0:T(8,128)}, u32[]{:S(2)}) copy-start(f32[4,64,8,128]{3,1,2,0:T(8,128)} %get-tuple-element.368) | copy-start | bytes 3145732
  441.8 32.3 %copy-start.131 = (f32[4,64,8,128]{3,1,2,0:T(8,128)S(1)}, f32[4,64,8,128]{3,1,2,0:T(8,128)}, u32[]{:S(2)}) copy-start(f32[4,64,8,128]{3,1,2,0:T(8,128)} %get-tuple-element.369) | copy-start | bytes 3145732
  441.8 32.3 %copy-start.132 = (f32[4,64,8,128]{3,1,2,0:T(8,128)S(1)}, f32[4,64,8,128]{3,1,2,0:T(8,128)}, u32[]{:S(2)}) copy-start(f32[4,64,8,128]{3,1,2,0:T(8,128)} %get-tuple-element.370) | copy-start | bytes 3145732
  441.8 32.3 %copy-start.144 = (f32[4,64,8,128]{3,1,2,0:T(8,128)S(1)}, f32[4,64,8,128]{3,1,2,0:T(8,128)}, u32[]{:S(2)}) copy-start(f32[4,64,8,128]{3,1,2,0:T(8,128)} %get-tuple-element.322) | copy-start | bytes 3145732
  441.8 32.3 %copy-start.145 = (f32[4,64,8,128]{3,1,2,0:T(8,128)S(1)}, f32[4,64,8,128]{3,1,2,0:T(8,128)}, u32[]{:S(2)}) copy-start(f32[4,64,8,128]{3,1,2,0:T(8,128)} %get-tuple-element.323) | copy-start | bytes 3145732
  441.8 32.3 %copy-start.146 = (f32[4,64,8,128]{3,1,2,0:T(8,128)S(1)}, f32[4,64,8,128]{3,1,2,0:T(8,128)}, u32[]{:S(2)}) copy-start(f32[4,64,8,128]{3,1,2,0:T(8,128)} %get-tuple-element.324) | copy-start | bytes 3145732
  531.9 9.3 %collective-permute-start.4 = (bf16[512,14,3]{0,2,1:T(4,128)(2,1)S(1)}, bf16[512,14,3]{0,2,1:T(4,128)(2,1)S(1)}, u32[]{:S(2)}, u32[]{:S(2)}) collective-permute-start(bf16[512,14,3]{0,2,1:T(4,128)(2,1)S(1)} %get-tuple-element.219), channel_id=1, source_target_pairs={{1,0},{2,1},{3,2},{4,3},{5,4},{6,5},{7,6},{8,7},{9,8},{10,9},{11,1... | collective-permute-start | bytes 129032 | tf_op jit(solution)/shard_map/ppermute | solution.py:31
  537.1 5.8 collective-permute-start.5
  548.3 9.4 %collective-permute-start.6 = (bf16[512,3,128]{0,2,1:T(8,128)(2,1)S(1)}, bf16[512,3,128]{0,2,1:T(8,128)(2,1)S(1)}, u32[]{:S(2)}, u32[]{:S(2)}) collective-permute-start(bf16[512,3,128]{0,2,1:T(8,128)(2,1)S(1)} %get-tuple-element.321), channel_id=1, source_target_pairs={{16,0},{32,16},{48,32},{64,48},{80,64},{96,80},{112,96},{17,1},{33... | collective-permute-start | bytes 1179656 | tf_op jit(solution)/shard_map/ppermute | solution.py:31
  551.2 8.3 %collective-permute-start.7 = (bf16[512,3,128]{0,2,1:T(8,128)(2,1)S(1)}, bf16[512,3,128]{0,2,1:T(8,128)(2,1)S(1)}, u32[]{:S(2)}, u32[]{:S(2)}) collective-permute-start(bf16[512,3,128]{0,2,1:T(8,128)(2,1)S(1)} %get-tuple-element.320), channel_id=1, source_target_pairs={{0,16},{16,32},{32,48},{48,64},{64,80},{80,96},{96,112},{1,17},{17... | collective-permute-start | bytes 1179656 | tf_op jit(solution)/shard_map/ppermute | solution.py:31
  (183 other events, 1148.0 us)
Sparse Core Ops, SparseCore 0:
  577.4 155.2 all-reduce.100
where the time goes:
time: 752 us; the launch traced here: 744 us
  local copies, waits for them, and re-layouts  331 us (44%)
  other arithmetic  193 us (26%)
  waiting for transfers between devices  162 us (22%)
  starting transfers between devices  23.7 us (3%)
  between operations  17.7 us (2%)
  matrix products  16.7 us (2%)
    unnamed x548, local copies, waits for them, and re-layouts  213 us
    psum x1, waiting for transfers between devices, per_device(): summed_wqkv, summed_wout = lax.psum((local_wqkv, grad_wout), ('row', 'col'))  154 us
    another operation x3, other arithmetic, per_device(): jnp.stack([grad_k_ext, grad_v_ext]).reshape(2 * depth, ext_rows, ext_cols)  67.7 us
    slice x3, local copies, waits for them, and re-layouts, value_at(): return value_ext[:, :, a:a + height, b:b + length].astype(jnp.float32)  28.5 us
    slice x3, local copies, waits for them, and re-layouts, key_at(): return key_ext[:, :, a:a + height, b:b + length].astype(jnp.float32)  27.9 us
    mul x3, other arithmetic, neighbor_pass(): slopes[i][:, None] * query32  22.2 us
    mul x3, other arithmetic, neighbor_pass(): weights[i][:, None] * grad_attn  20.8 us
    reduce_sum x3, other arithmetic, norm_back(): inner = jnp.mean(grad * raw, axis=-3, keepdims=True)  18.4 us
  transfers between devices with their start and end apart: 9, of which 5 were waited for; matrix products, arithmetic and copies ran while one was open for 3% of the time, Pallas kernels for 0%

commit v1 on v0

v1 whole, which is shorter than its diff:
```python
import collections
import functools
import math

import jax
import jax.numpy as jnp
from jax import lax
from jax.experimental import pallas as pl
from jax.experimental.pallas import tpu as pltpu
from jax.sharding import PartitionSpec as P

MESH = pl.DeviceIdType.MESH
F32 = jnp.float32
BF16 = jnp.bfloat16

D = 256
HEADS = 4
HW = 64
RADIUS = 3
EPS = 1e-06
H = 8
W = 128
B = 16
NB = W // B
NG = NB + 1
ER = 16
GC = ER * B
WT = 4 * D

DIRS = ((-1, 0), (1, 0), (0, -1), (0, 1), (-1, -1), (-1, 1), (1, -1), (1, 1))


def dot(a, b):
    return lax.dot_general(a, b, (((1,), (0,)), ((), ())), preferred_element_type=F32)


def dot_nt(a, b):
    return lax.dot_general(a, b, (((1,), (1,)), ((), ())), preferred_element_type=F32)


def heads(x):
    return x.reshape(HEADS, HW, x.shape[-1])


def flat(x):
    return x.reshape(HEADS * HW, x.shape[-1])


def scratch_shapes(nr, nc):
    cc = 2 * D // nc
    return collections.OrderedDict(
        l32=pltpu.VMEM((D * H, W), F32),
        g32=pltpu.VMEM((D * H, W), F32),
        inv=pltpu.VMEM((H, W), F32),
        xr=pltpu.VMEM((H * W, D), BF16),
        xe32=pltpu.VMEM((2, H * 8, D), F32),
        xe=pltpu.VMEM((2, H * 8, D), BF16),
        rx_row=pltpu.VMEM((2, RADIUS * W, D), BF16),
        rx_col=pltpu.VMEM((2, H * 8, D), BF16),
        rx_cor=pltpu.VMEM((4, 32, D), BF16),
        xg=pltpu.VMEM((NG, GC, D), BF16),
        xb=pltpu.VMEM((NB, H * B, D), BF16),
        gob=pltpu.VMEM((NB, H * B, D), BF16),
        wot=pltpu.VMEM((D, D), BF16),
        wt=pltpu.VMEM((D, 3 * D), BF16),
        kraw=pltpu.VMEM((NG, D, GC), F32),
        kinv=pltpu.VMEM((NG, HEADS, 1, GC), F32),
        kc=pltpu.VMEM((NG, GC, D), BF16),
        vc=pltpu.VMEM((NG, GC, D), BF16),
        kt=pltpu.VMEM((NG, D, GC), BF16),
        vt=pltpu.VMEM((NG, D, GC), BF16),
        qraw=pltpu.VMEM((NB, D, H * B), F32),
        qinv=pltpu.VMEM((NB, HEADS, 1, H * B), F32),
        qm=pltpu.VMEM((NB, 2, 2 * HW, 2 * H * B), BF16),
        gm=pltpu.VMEM((NB, 2, 2 * HW, 2 * H * B), BF16),
        mask=pltpu.VMEM((3, 2 * GC, H * B), F32),
        gk=pltpu.VMEM((NG, D, GC), F32),
        gv=pltpu.VMEM((NG, D, GC), F32),
        gq=pltpu.VMEM((NB, D, H * B), F32),
        at=pltpu.VMEM((NB, D, H * B), BF16),
        gqb=pltpu.VMEM((NB, D, H * B), BF16),
        gkv=pltpu.VMEM((NG, 2 * D, GC), BF16),
        gn=pltpu.VMEM((2 * RADIUS + H, NG * B, D), F32),
        tx_row=pltpu.VMEM((2, RADIUS * W, D), BF16),
        tx_col=pltpu.VMEM((2, H * 8, D), BF16),
        tx_cor=pltpu.VMEM((4, 32, D), BF16),
        ry_row=pltpu.VMEM((2, RADIUS * W, D), BF16),
        ry_col=pltpu.VMEM((2, H * 8, D), BF16),
        ry_cor=pltpu.VMEM((4, 32, D), BF16),
        wg=pltpu.VMEM((WT, D), F32),
        wb=pltpu.VMEM((WT, D), BF16),
        rx_half=pltpu.VMEM((WT // 2, D), BF16),
        half=pltpu.VMEM((WT // 2, D), F32),
        hb=pltpu.VMEM((WT // 2, D), BF16),
        rx_pl=pltpu.VMEM((nc, cc, D), BF16),
        ys=pltpu.VMEM((nr // 2, cc, D), F32),
        fb=pltpu.VMEM((WT, D), BF16),
        s_hal=pltpu.SemaphoreType.DMA((8,)),
        r_hal=pltpu.SemaphoreType.DMA((8,)),
        s_ret=pltpu.SemaphoreType.DMA((8,)),
        r_ret=pltpu.SemaphoreType.DMA((8,)),
        s_core=pltpu.SemaphoreType.DMA((2,)),
        r_core=pltpu.SemaphoreType.DMA((2,)),
        s_pl=pltpu.SemaphoreType.DMA((2, nc)),
        r_pl=pltpu.SemaphoreType.DMA((2, nc)),
        s_y=pltpu.SemaphoreType.DMA((nr // 2,)),
        r_y=pltpu.SemaphoreType.DMA((nr // 2,)),
    )


def kernel(nr, nc, names, *refs):
    S = collections.namedtuple("S", names)(*refs)
    row, col = lax.axis_index("row"), lax.axis_index("col")
    core, ypos = lax.rem(row, 2), lax.div(row, 2)
    ny = nr // 2
    cc = 2 * D // nc

    def at(dr, dc):
        return (lax.rem(row + (dr % nr), nr), lax.rem(col + (dc % nc), nc))

    mate = (row + 1 - 2 * core, col)

    def remote(src, dst, send, recv, device):
        return pltpu.make_async_remote_copy(
            src_ref=src, dst_ref=dst, send_sem=send, recv_sem=recv, device_id=device, device_id_type=MESH
        )

    partners = list(DIRS)
    partners += [(0, k) for k in range(2, nc - 1)]
    partners += [(2 * m, 0) for m in range(1, ny)]
    barrier = pltpu.get_barrier_semaphore()
    for dr, dc in partners:
        pl.semaphore_signal(barrier, inc=1, device_id=at(dr, dc), device_id_type=MESH)

    step = 32

    def load(i, acc):
        x = S.lat[pl.ds(i * step, step)].astype(F32)
        S.l32[pl.ds(pl.multiple_of(i * step * H, step * H), step * H), :] = x.reshape(step * H, W)
        g = S.go[pl.ds(i * step, step)].astype(F32)
        S.g32[pl.ds(pl.multiple_of(i * step * H, step * H), step * H), :] = g.reshape(step * H, W)
        return acc + jnp.sum(x * x, axis=0)

    total = lax.fori_loop(0, D // step, load, jnp.zeros((H, W), F32))
    S.inv[...] = lax.rsqrt(total * (1.0 / D) + EPS)
    gain = S.gain[...]

    def cells(r, carry):
        x = S.l32[pl.ds(r, D, stride=H), :] * S.inv[pl.ds(r, 1), :]
        xn = x.T * gain
        xnb = xn.astype(BF16)
        S.xr[pl.ds(pl.multiple_of(r * W, W), W), :] = xnb
        S.xe32[0, pl.ds(pl.multiple_of(r * 8, 8), 8), :] = xn[:8]
        S.xe32[1, pl.ds(pl.multiple_of(r * 8, 8), 8), :] = xn[W - 8 :]
        own = pl.ds(pl.multiple_of(r * B, B), B)
        ext = pl.ds(pl.multiple_of(r * B + RADIUS * B, B), B)
        for j in range(NB):
            S.xb[j, own, :] = xnb[j * B : (j + 1) * B]
        for g in range(1, NB):
            S.xg[g, ext, :] = xn[g * B - 8 : g * B + 8].astype(BF16)
        return carry

    lax.fori_loop(0, H, cells, 0)
    S.xe[...] = S.xe32[...].astype(BF16)

    pl.semaphore_wait(barrier, len(partners))
    near = 3 * W
    edge = {-1: slice(0, near), 1: slice(H * W - near, H * W)}
    part = {-1: slice(0, 32), 1: slice(32, 64)}
    halo = []
    for i, (dr, dc) in enumerate(DIRS):
        if dc == 0:
            src, dst = S.xr.at[edge[dr]], S.rx_row.at[i]
        elif dr == 0:
            src, dst = S.xe.at[(dc + 1) // 2], S.rx_col.at[i - 2]
        else:
            src, dst = S.xe.at[(dc + 1) // 2, part[dr]], S.rx_cor.at[i - 4]
        halo.append(remote(src, dst, S.s_hal.at[i], S.r_hal.at[i], at(dr, dc)))
        halo[-1].start()

    S.wot[...] = S.wo[...].T
    for i in range(3):
        S.wt[:, i * D : (i + 1) * D] = S.wqkv[i * D : (i + 1) * D, :].T

    def grads(r, carry):
        g = S.g32[pl.ds(r, D, stride=H), :].T.astype(BF16)
        own = pl.ds(pl.multiple_of(r * B, B), B)
        for j in range(NB):
            S.gob[j, own, :] = g[j * B : (j + 1) * B]
        return carry

    lax.fori_loop(0, H, grads, 0)

    mshape = (2, ER, B, H * B)
    half_, kr, kc = (lax.broadcasted_iota(jnp.int32, mshape, a) for a in range(3))
    lane = lax.broadcasted_iota(jnp.int32, mshape, 3)
    qr, qc = lax.div(lane, B), lax.rem(lane, B)
    dr = kr - RADIUS - qr
    off = B * half_ + kc - 8
    dc = off - qc
    grow = row * H + kr - RADIUS
    ok = (dr >= -RADIUS) & (dr <= RADIUS) & (dc >= -RADIUS) & (dc <= RADIUS)
    ok = ok & (grow >= 0) & (grow < nr * H)
    one = jnp.where(ok, 1.0, 0.0).astype(F32).reshape(2 * GC, H * B)
    off = off.reshape(2 * GC, H * B)
    S.mask[0] = jnp.where((col * W + off >= 0), one, 0.0)
    S.mask[1] = one
    S.mask[2] = jnp.where(col * W + W - B + off < nc * W, one, 0.0)

    def queries(j, carry):
        q = heads(dot_nt(S.wqkv[0:D, :], S.xb[j]))
        inv = lax.rsqrt(jnp.mean(q * q, axis=1, keepdims=True) + EPS)
        qn = (q * inv).astype(BF16)
        S.qraw[j] = flat(q)
        S.qinv[j] = inv
        ga = heads(dot_nt(S.wot[...], S.gob[j])).astype(BF16)
        z = jnp.zeros((HW, H * B), BF16)
        for p in range(2):
            for x, out in ((qn, S.qm), (ga, S.gm)):
                out[j, p, 0:HW, :] = jnp.concatenate([x[2 * p], z], axis=1)
                out[j, p, HW : 2 * HW, :] = jnp.concatenate([z, x[2 * p + 1]], axis=1)
        return carry

    lax.fori_loop(0, NB, queries, 0)

    for c in halo:
        c.wait_recv()
    left = S.rx_col[1].astype(F32)
    right = S.rx_col[0].astype(F32)

    def ends(er, cells_, l8, r8):
        S.xg[0, er * B : (er + 1) * B, :] = jnp.concatenate([l8, cells_[:8]], axis=0).astype(BF16)
        S.xg[NB, er * B : (er + 1) * B, :] = jnp.concatenate([cells_[-8:], r8], axis=0).astype(BF16)

    for r in range(H):
        ends(
            r + RADIUS,
            jnp.concatenate([S.xe32[0, r * 8 : r * 8 + 8, :], S.xe32[1, r * 8 : r * 8 + 8, :]], axis=0),
            left[r * 8 : r * 8 + 8],
            right[r * 8 : r * 8 + 8],
        )
    for up in (0, 1):
        l_cor = S.rx_cor[2 * up + 1].astype(F32)
        r_cor = S.rx_cor[2 * up].astype(F32)
        for i in range(RADIUS):
            er = i if up == 1 else RADIUS + H + i
            at_cor = (i + 1) * 8 if up == 1 else i * 8
            line = S.rx_row[up, i * W : (i + 1) * W, :].astype(F32)
            for g in range(1, NB):
                S.xg[g, er * B : (er + 1) * B, :] = line[g * B - 8 : g * B + 8].astype(BF16)
            ends(er, line, l_cor[at_cor : at_cor + 8], r_cor[at_cor : at_cor + 8])
    for g in range(NG):
        S.xg[g, (2 * RADIUS + H) * B :, :] = jnp.zeros((2 * B, D), BF16)

    def pairs(g, carry):
        kv = dot_nt(S.wqkv[D : 3 * D, :], S.xg[g])
        k = heads(kv[:D])
        inv = lax.rsqrt(jnp.mean(k * k, axis=1, keepdims=True) + EPS)
        kn = flat(k * inv).astype(BF16)
        v = kv[D:].astype(BF16)
        S.kraw[g] = kv[:D]
        S.kinv[g] = inv
        S.kt[g] = kn
        S.vt[g] = v
        S.kc[g] = kn.T
        S.vc[g] = v.T
        return carry

    lax.fori_loop(0, NG, pairs, 0)

    S.gk[0] = jnp.zeros((D, GC), F32)
    S.gv[0] = jnp.zeros((D, GC), F32)
    factor = [S.cos[h] * (1.0 / HW) for h in range(HEADS)]
    lg = [f * math.log2(math.e) for f in factor]

    def attention(j, carry):
        which = jnp.where(j == 0, 0, jnp.where(j == NB - 1, 2, 1))
        for p in range(2):
            ch = slice(p * 2 * HW, (p + 1) * 2 * HW)
            qm, gm = S.qm[j, p], S.gm[j, p]
            keys = jnp.concatenate([S.kc[j, :, ch], S.kc[j + 1, :, ch]], axis=0)
            vals = jnp.concatenate([S.vc[j, :, ch], S.vc[j + 1, :, ch]], axis=0)
            score = dot(keys, qm)
            prod = dot(vals, gm)
            probs, slopes = [], []
            for i in range(2):
                lanes = slice(i * H * B, (i + 1) * H * B)
                e = jnp.exp2(score[:, lanes] * lg[2 * p + i]) * S.mask[which]
                w = e * (1.0 / jnp.sum(e, axis=0, keepdims=True))
                wd = w * prod[:, lanes]
                s = wd - w * jnp.sum(wd, axis=0, keepdims=True)
                probs.append(w.astype(BF16))
                slopes.append(s.astype(BF16))
            prob = jnp.concatenate(probs, axis=1)
            slope = jnp.concatenate(slopes, axis=1)
            keys_t = jnp.concatenate([S.kt[j, ch, :], S.kt[j + 1, ch, :]], axis=1)
            vals_t = jnp.concatenate([S.vt[j, ch, :], S.vt[j + 1, ch, :]], axis=1)
            attn = dot(vals_t, prob)
            grad_q = dot(keys_t, slope)
            for i in range(2):
                lanes = slice(i * H * B, (i + 1) * H * B)
                c = slice(i * HW, (i + 1) * HW)
                o = slice((2 * p + i) * HW, (2 * p + i + 1) * HW)
                S.at[j, o, :] = attn[c, lanes].astype(BF16)
                S.gq[j, o, :] = grad_q[c, lanes] * factor[2 * p + i]
            grad_k = dot_nt(qm, slope)
            grad_v = dot_nt(gm, prob)
            S.gk[j, ch, :] += grad_k[:, :GC]
            S.gk[j + 1, ch, :] = grad_k[:, GC:]
            S.gv[j, ch, :] += grad_v[:, :GC]
            S.gv[j + 1, ch, :] = grad_v[:, GC:]
        return carry

    lax.fori_loop(0, NB, attention, 0)

    def norm_back(raw, inv, grad):
        inner = jnp.mean(grad * raw, axis=1, keepdims=True)
        return inv * (grad - raw * (inv * inv * inner))

    S.wg[...] = jnp.zeros((WT, D), F32)

    def back_q(j, carry):
        g = flat(norm_back(heads(S.qraw[j]), S.qinv[j], heads(S.gq[j]))).astype(BF16)
        S.gqb[j] = g
        S.wg[0:D, :] += dot(g, S.xb[j])
        S.wg[3 * D :, :] += dot(S.at[j], S.gob[j])
        return carry

    lax.fori_loop(0, NB, back_q, 0)
    S.wg[3 * D :, :] = S.wg[3 * D :, :].T

    def back_kv(g, carry):
        gk = heads(S.gk[g])
        gk = jnp.concatenate([gk[h : h + 1] * factor[h] for h in range(HEADS)], axis=0)
        gk = flat(norm_back(heads(S.kraw[g]), S.kinv[g], gk)).astype(BF16)
        gkv = jnp.concatenate([gk, S.gv[g].astype(BF16)], axis=0)
        S.gkv[g] = gkv
        S.wg[D : 3 * D, :] += dot(gkv, S.xg[g])
        return carry

    lax.fori_loop(0, NG, back_kv, 0)

    hw = WT // 2
    S.wb[...] = S.wg[...].astype(BF16)
    mine = pl.ds(pl.multiple_of(core * hw, hw), hw)
    other = pl.ds(pl.multiple_of((1 - core) * hw, hw), hw)
    to_mate = remote(S.wb.at[other], S.rx_half, S.s_core.at[0], S.r_core.at[0], mate)
    to_mate.start()

    def cells_kv(g, carry):
        x = dot(S.wt[:, D:], S.gkv[g]).T
        for er in range(2 * RADIUS + H):
            S.gn[er, pl.ds(pl.multiple_of(g * B, B), B), :] = x[er * B : (er + 1) * B]
        return carry

    lax.fori_loop(0, NG, cells_kv, 0)

    low, high = 8, 8 + W
    rows_at = {-1: 0, 1: RADIUS + H}
    cols_at = {-1: slice(0, 8), 1: slice(high, high + 8)}
    back = []
    for i, (dr, dc) in enumerate(DIRS):
        if dc == 0:
            a = rows_at[dr]
            S.tx_row[i] = S.gn[a : a + RADIUS, low:high, :].reshape(RADIUS * W, D).astype(BF16)
            src, dst = S.tx_row.at[i], S.ry_row.at[i]
        elif dr == 0:
            S.tx_col[i - 2] = S.gn[RADIUS : RADIUS + H, cols_at[dc], :].reshape(H * 8, D).astype(BF16)
            src, dst = S.tx_col.at[i - 2], S.ry_col.at[i - 2]
        else:
            a = rows_at[dr]
            cor = S.gn[a : a + RADIUS, cols_at[dc], :].reshape(RADIUS * 8, D)
            S.tx_cor[i - 4] = jnp.concatenate([cor, jnp.zeros((8, D), F32)], axis=0).astype(BF16)
            src, dst = S.tx_cor.at[i - 4], S.ry_cor.at[i - 4]
        back.append(remote(src, dst, S.s_ret.at[i], S.r_ret.at[i], at(dr, dc)))
        back[-1].start()

    to_mate.wait_recv()
    half = S.wg[mine, :] + S.rx_half[...].astype(F32)
    S.half[...] = half
    S.hb[...] = half.astype(BF16)
    scatter = []
    for k in range(1, nc):
        t = lax.rem(col + k, nc)
        scatter.append(
            remote(
                S.hb.at[pl.ds(pl.multiple_of(t * cc, cc), cc)],
                S.rx_pl.at[k],
                S.s_pl.at[0, k],
                S.r_pl.at[0, k],
                (row, t),
            )
        )
        scatter[-1].start()

    def cells_q(j, carry):
        x = dot(S.wt[:, 0:D], S.gqb[j]).T
        for r in range(H):
            S.gn[RADIUS + r, pl.ds(pl.multiple_of(j * B + 8, 8), B), :] += x[r * B : (r + 1) * B]
        return carry

    lax.fori_loop(0, NB, cells_q, 0)

    for c in scatter:
        c.wait_recv()
    chunk = S.half[pl.ds(pl.multiple_of(col * cc, cc), cc), :]
    for k in range(1, nc):
        chunk = chunk + S.rx_pl[k].astype(F32)
    S.ys[ypos] = chunk
    over_y = []
    for m in range(1, ny):
        over_y.append(remote(S.ys.at[ypos], S.ys.at[ypos], S.s_y.at[m], S.r_y.at[m], at(2 * m, 0)))
        over_y[-1].start()

    for c in back:
        c.wait_recv()
    first, last = RADIUS, RADIUS + H - RADIUS
    S.gn[last : last + RADIUS, low:high, :] += S.ry_row[0].astype(F32).reshape(RADIUS, W, D)
    S.gn[first : first + RADIUS, low:high, :] += S.ry_row[1].astype(F32).reshape(RADIUS, W, D)
    S.gn[first : first + H, high - 8 : high, :] += S.ry_col[0].astype(F32).reshape(H, 8, D)
    S.gn[first : first + H, low : low + 8, :] += S.ry_col[1].astype(F32).reshape(H, 8, D)
    for i, (dr, dc) in enumerate(DIRS[4:]):
        a = last if dr == -1 else first
        b = high - 8 if dc == -1 else low
        cor = S.ry_cor[i].astype(F32)[: RADIUS * 8]
        S.gn[a : a + RADIUS, b : b + 8, :] += cor.reshape(RADIUS, 8, D)

    for c in over_y:
        c.wait_recv()
    chunk = S.ys[0]
    for m in range(1, ny):
        chunk = chunk + S.ys[m]
    chunk = chunk * (1.0 / math.sqrt(nr * H * nc * W))
    place = pl.ds(pl.multiple_of(core * hw + col * cc, cc), cc)
    S.fb[place, :] = chunk.astype(BF16)
    gather = []
    for k in range(1, nc):
        gather.append(
            remote(
                S.fb.at[place],
                S.fb.at[place],
                S.s_pl.at[1, k],
                S.r_pl.at[1, k],
                at(0, k),
            )
        )
        gather[-1].start()

    def last_norm(r, carry):
        g = (S.gn[RADIUS + r, low:high, :] * gain).T
        x = S.l32[pl.ds(r, D, stride=H), :]
        inv = S.inv[pl.ds(r, 1), :]
        inner = jnp.mean(g * x, axis=0, keepdims=True)
        S.l32[pl.ds(r, D, stride=H), :] = inv * (g - x * (inv * inv * inner))
        return carry

    lax.fori_loop(0, H, last_norm, 0)

    def store(i, carry):
        x = S.l32[pl.ds(pl.multiple_of(i * step * H, step * H), step * H), :]
        S.gl[pl.ds(i * step, step)] = x.reshape(step, H, W).astype(BF16)
        return carry

    lax.fori_loop(0, D // step, store, 0)

    for c in gather:
        c.wait_recv()
    done = remote(S.fb.at[mine], S.fb.at[mine], S.s_core.at[1], S.r_core.at[1], mate)
    done.start()
    done.wait_recv()
    S.gwqkv[...] = S.fb[0 : 3 * D, :].astype(F32)
    S.gwo[...] = S.fb[3 * D :, :].astype(F32)

    for c in halo + back + scatter + over_y + gather + [to_mate, done]:
        c.wait_send()


def solution(mesh):
    nr, nc = mesh.shape["row"], mesh.shape["col"]
    scratch = scratch_shapes(nr, nc)
    names = ["lat", "gain", "wqkv", "wo", "cos", "go", "gl", "gwqkv", "gwo", *scratch]

    def per_device(latent, norm_gain, qkv_weight, out_weight, cos_scale, grad_output):
        vmem = pl.BlockSpec(memory_space=pltpu.VMEM)
        return pl.pallas_call(
            functools.partial(kernel, nr, nc, names),
            out_shape=(
                jax.ShapeDtypeStruct((D, H, W), BF16),
                jax.ShapeDtypeStruct((3 * D, D), F32),
                jax.ShapeDtypeStruct((D, D), F32),
            ),
            in_specs=[vmem, vmem, vmem, vmem, pl.BlockSpec(memory_space=pltpu.SMEM), vmem],
            out_specs=(vmem, vmem, vmem),
            scratch_shapes=list(scratch.values()),
            compiler_params=pltpu.CompilerParams(
                collective_id=0, has_side_effects=True, vmem_limit_bytes=60 * 2**20
            ),
        )(latent, norm_gain.reshape(1, D), qkv_weight, out_weight, cos_scale, grad_output)

    return jax.shard_map(
        per_device,
        mesh=mesh,
        in_specs=(P(None, "row", "col"), P(), P(), P(), P(), P(None, "row", "col")),
        out_specs=(P(None, "row", "col"), P(), P()),
        check_vma=False,
    )
```

time: 752 us -> 62.5 us (0.08); the launches traced: 744 us -> 62.3 us
  local copies, waits for them, and re-layouts: 331 us -> 3.74 us
  other arithmetic: 193 us -> 0 us
  waiting for transfers between devices: 162 us -> 0 us
  Pallas kernels: 0 us -> 57.9 us
  starting transfers between devices: 23.7 us -> 0 us
  between operations: 17.7 us -> 0.65 us
  matrix products: 16.7 us -> 0 us
    unnamed x548 -> x7, local copies, waits for them, and re-layouts: 213 us -> 3.74 us
    psum x1 -> x0, waiting for transfers between devices: 154 us -> none  [per_device(): summed_wqkv, summed_wout = lax.psum((local_wqkv, grad_wout), ('row', 'col'))]
    slice x25 -> x0, local copies, waits for them, and re-layouts: 81 us -> none  [the longest x3 28.5 us: value_at(): return value_ext[:, :, a:a + height, b:b + length].astype(jnp.float32)]
    another operation x7 -> x0, other arithmetic: 72.8 us -> none  [the longest x3 67.7 us: per_device(): jnp.stack([grad_k_ext, grad_v_ext]).reshape(2 * depth, ext_rows, ext_cols)]
    pallas_call x0 -> x1, Pallas kernels: none -> 57.9 us  [per_device(): pl.pallas_call(functools.partial(kernel, nr, nc, names), out_shape=(jax.S...]
    mul x17 -> x0, other arithmetic: 54.7 us -> none  [the longest x3 22.2 us: neighbor_pass(): slopes[i][:, None] * query32]
    reduce_sum x11 -> x0, other arithmetic: 39.5 us -> none  [the longest x3 18.4 us: norm_back(): inner = jnp.mean(grad * raw, axis=-3, keepdims=True)]
    ppermute x8 -> x0, starting transfers between devices: 23.7 us -> none  [the longest x4 11.5 us: shifted(): return lax.ppermute(shard, axis, pairs)]
  transfers between devices with their start and end apart: 9 -> 0, of which waited for: 5 -> 0; matrix products, arithmetic and copies ran while one was open for 3% -> 0% of each run, Pallas kernels for 0% -> 0%
where the time goes in v1:
time: 62.5 us; the launch traced here: 62.3 us
  Pallas kernels  57.9 us (93%)
  local copies, waits for them, and re-layouts  3.74 us (6%)
  between operations  0.65 us (1%)
    pallas_call x1, Pallas kernels, per_device(): pl.pallas_call(functools.partial(kernel, nr, nc, names), out_shape=(jax.S...  57.9 us
    unnamed x7, local copies, waits for them, and re-layouts  3.74 us

profile of v1, /device:TPU:1, one launch (start us, length us, event | category | flops | bytes accessed | tf_op | source)
XLA Modules:
  0.0 62.3 jit_solution(9667977505079816300)
XLA Ops:
  0.6 57.9 %shard_map.85 = (bf16[256,8,128]{2,1,0:T(8,128)(2,1)}, f32[768,256]{1,0:T(8,128)}, f32[256,256]{1,0:T(8,128)}) custom-call(bf16[256,8,128]{2,1,0:T(8,128)(2,1)} %refs_0_.1, f32[1,256]{1,0:T(1,128)} %bitcast.1, bf16[768,256]{1,0:T(8,128)(2,1)} %refs_2_.1, bf16[256,256]{1,0:T(8,128)(2,1)} %refs_3_.1, f32[4]{0:T(128)} %refs_4_.1, bf16[256,8,128]{2,1,0:T(8,128)(2,1)} %refs_5_.1), custom_call_target="tpu_custom_call" | custom-call | tf_op jit(solution)/shard_map/pallas_call | solution.py:485
  58.5 0.0 copy-start
  58.5 1.9 %copy.12 = bf16[256,8,128]{2,1,0:T(8,128)(2,1)} copy(bf16[256,8,128]{2,1,0:T(8,128)(2,1)} %get-tuple-element.6) | data formatting | bytes 1048576
  60.5 0.0 copy-done
  60.5 0.0 copy-start.1
  60.5 0.9 %copy.13 = f32[768,256]{1,0:T(8,128)} copy(f32[768,256]{1,0:T(8,128)S(1)} %copy-done) | data formatting | bytes 1572864
  61.4 0.2 copy-done.1
  61.6 0.7 %copy.14 = f32[256,256]{1,0:T(8,128)} copy(f32[256,256]{1,0:T(8,128)S(1)} %copy-done.1) | data formatting | bytes 524288
Async XLA Ops:
  58.5 2.0 %copy-start = (f32[768,256]{1,0:T(8,128)S(1)}, f32[768,256]{1,0:T(8,128)}, u32[]{:S(2)}) copy-start(f32[768,256]{1,0:T(8,128)} %get-tuple-element.7) | copy-start | bytes 2359300
  60.5 1.1 %copy-start.1 = (f32[256,256]{1,0:T(8,128)S(1)}, f32[256,256]{1,0:T(8,128)}, u32[]{:S(2)}) copy-start(f32[256,256]{1,0:T(8,128)} %get-tuple-element.8) | copy-start | bytes 786436

commit v2 on v1

--- a/solution.py
+++ b/solution.py
@@ -26,6 +26,7 @@
 ER = 16
 GC = ER * B
 WT = 4 * D
+CHUNK = 64
 
 DIRS = ((-1, 0), (1, 0), (0, -1), (0, 1), (-1, -1), (-1, 1), (1, -1), (1, 1))
 
@@ -74,6 +75,8 @@
         qm=pltpu.VMEM((NB, 2, 2 * HW, 2 * H * B), BF16),
         gm=pltpu.VMEM((NB, 2, 2 * HW, 2 * H * B), BF16),
         mask=pltpu.VMEM((3, 2 * GC, H * B), F32),
+        eb=pltpu.VMEM((2, 2 * GC, 2 * H * B), BF16),
+        sb=pltpu.VMEM((2, 2 * GC, 2 * H * B), BF16),
         gk=pltpu.VMEM((NG, D, GC), F32),
         gv=pltpu.VMEM((NG, D, GC), F32),
         gq=pltpu.VMEM((NB, D, H * B), F32),
@@ -160,7 +163,7 @@
             S.xg[g, ext, :] = xn[g * B - 8 : g * B + 8].astype(BF16)
         return carry
 
-    lax.fori_loop(0, H, cells, 0)
+    lax.fori_loop(0, H, cells, 0, unroll=True)
     S.xe[...] = S.xe32[...].astype(BF16)
 
     pl.semaphore_wait(barrier, len(partners))
@@ -189,7 +192,7 @@
             S.gob[j, own, :] = g[j * B : (j + 1) * B]
         return carry
 
-    lax.fori_loop(0, H, grads, 0)
+    lax.fori_loop(0, H, grads, 0, unroll=True)
 
     mshape = (2, ER, B, H * B)
     half_, kr, kc = (lax.broadcasted_iota(jnp.int32, mshape, a) for a in range(3))
@@ -221,7 +224,7 @@
                 out[j, p, HW : 2 * HW, :] = jnp.concatenate([z, x[2 * p + 1]], axis=1)
         return carry
 
-    lax.fori_loop(0, NB, queries, 0)
+    lax.fori_loop(0, NB, queries, 0, unroll=True)
 
     for c in halo:
         c.wait_recv()
@@ -266,7 +269,7 @@
         S.vc[g] = v.T
         return carry
 
-    lax.fori_loop(0, NG, pairs, 0)
+    lax.fori_loop(0, NG, pairs, 0, unroll=True)
 
     S.gk[0] = jnp.zeros((D, GC), F32)
     S.gv[0] = jnp.zeros((D, GC), F32)
@@ -275,43 +278,55 @@
 
     def attention(j, carry):
         which = jnp.where(j == 0, 0, jnp.where(j == NB - 1, 2, 1))
+        st = []
         for p in range(2):
             ch = slice(p * 2 * HW, (p + 1) * 2 * HW)
             qm, gm = S.qm[j, p], S.gm[j, p]
             keys = jnp.concatenate([S.kc[j, :, ch], S.kc[j + 1, :, ch]], axis=0)
             vals = jnp.concatenate([S.vc[j, :, ch], S.vc[j + 1, :, ch]], axis=0)
-            score = dot(keys, qm)
-            prod = dot(vals, gm)
-            probs, slopes = [], []
-            for i in range(2):
-                lanes = slice(i * H * B, (i + 1) * H * B)
-                e = jnp.exp2(score[:, lanes] * lg[2 * p + i]) * S.mask[which]
-                w = e * (1.0 / jnp.sum(e, axis=0, keepdims=True))
-                wd = w * prod[:, lanes]
-                s = wd - w * jnp.sum(wd, axis=0, keepdims=True)
-                probs.append(w.astype(BF16))
-                slopes.append(s.astype(BF16))
-            prob = jnp.concatenate(probs, axis=1)
-            slope = jnp.concatenate(slopes, axis=1)
+            st.append((dot(keys, qm), dot(vals, gm)))
+        for p in range(2):
+            ch = slice(p * 2 * HW, (p + 1) * 2 * HW)
+            qm, gm = S.qm[j, p], S.gm[j, p]
+            score, prod = st[p]
+            lgr = jnp.concatenate([jnp.full((1, H * B), lg[2 * p + i], F32) for i in range(2)], axis=1)
+            far = jnp.concatenate([jnp.full((1, H * B), factor[2 * p + i], F32) for i in range(2)], axis=1)
+            tot = jnp.zeros((8, 2 * H * B), F32)
+            ed = jnp.zeros((8, 2 * H * B), F32)
+            for c in range(0, 2 * GC, CHUNK):
+                mk = S.mask[which, c : c + CHUNK, :]
+                e = jnp.exp2(score[c : c + CHUNK] * lgr) * jnp.concatenate([mk, mk], axis=1)
+                tot = tot + jnp.sum(e.reshape(CHUNK // 8, 8, 2 * H * B), axis=0)
+                ed = ed + jnp.sum((e * prod[c : c + CHUNK]).reshape(CHUNK // 8, 8, 2 * H * B), axis=0)
+                S.eb[p, c : c + CHUNK, :] = e.astype(BF16)
+            rt = 1.0 / jnp.sum(tot, axis=0, keepdims=True)
+            m = jnp.sum(ed, axis=0, keepdims=True) * rt
+            for c in range(0, 2 * GC, CHUNK):
+                e = S.eb[p, c : c + CHUNK, :].astype(F32)
+                S.sb[p, c : c + CHUNK, :] = (e * (prod[c : c + CHUNK] - m)).astype(BF16)
+            prob = S.eb[p]
+            slope = S.sb[p]
             keys_t = jnp.concatenate([S.kt[j, ch, :], S.kt[j + 1, ch, :]], axis=1)
             vals_t = jnp.concatenate([S.vt[j, ch, :], S.vt[j + 1, ch, :]], axis=1)
-            attn = dot(vals_t, prob)
-            grad_q = dot(keys_t, slope)
+            attn = dot(vals_t, prob) * rt
+            grad_q = dot(keys_t, slope) * (rt * far)
             for i in range(2):
                 lanes = slice(i * H * B, (i + 1) * H * B)
                 c = slice(i * HW, (i + 1) * HW)
                 o = slice((2 * p + i) * HW, (2 * p + i + 1) * HW)
                 S.at[j, o, :] = attn[c, lanes].astype(BF16)
-                S.gq[j, o, :] = grad_q[c, lanes] * factor[2 * p + i]
-            grad_k = dot_nt(qm, slope)
-            grad_v = dot_nt(gm, prob)
+                S.gq[j, o, :] = grad_q[c, lanes]
+            qs = (qm.astype(F32) * rt).astype(BF16)
+            gs = (gm.astype(F32) * rt).astype(BF16)
+            grad_k = dot_nt(qs, slope)
+            grad_v = dot_nt(gs, prob)
             S.gk[j, ch, :] += grad_k[:, :GC]
             S.gk[j + 1, ch, :] = grad_k[:, GC:]
             S.gv[j, ch, :] += grad_v[:, :GC]
             S.gv[j + 1, ch, :] = grad_v[:, GC:]
         return carry
 
-    lax.fori_loop(0, NB, attention, 0)
+    lax.fori_loop(0, NB, attention, 0, unroll=2)
 
     def norm_back(raw, inv, grad):
         inner = jnp.mean(grad * raw, axis=1, keepdims=True)
@@ -326,7 +341,7 @@
         S.wg[3 * D :, :] += dot(S.at[j], S.gob[j])
         return carry
 
-    lax.fori_loop(0, NB, back_q, 0)
+    lax.fori_loop(0, NB, back_q, 0, unroll=True)
     S.wg[3 * D :, :] = S.wg[3 * D :, :].T
 
     def back_kv(g, carry):
@@ -338,7 +353,7 @@
         S.wg[D : 3 * D, :] += dot(gkv, S.xg[g])
         return carry
 
-    lax.fori_loop(0, NG, back_kv, 0)
+    lax.fori_loop(0, NG, back_kv, 0, unroll=True)
 
     hw = WT // 2
     S.wb[...] = S.wg[...].astype(BF16)
@@ -353,7 +368,7 @@
             S.gn[er, pl.ds(pl.multiple_of(g * B, B), B), :] = x[er * B : (er + 1) * B]
         return carry
 
-    lax.fori_loop(0, NG, cells_kv, 0)
+    lax.fori_loop(0, NG, cells_kv, 0, unroll=True)
 
     low, high = 8, 8 + W
     rows_at = {-1: 0, 1: RADIUS + H}
@@ -399,7 +414,7 @@
             S.gn[RADIUS + r, pl.ds(pl.multiple_of(j * B + 8, 8), B), :] += x[r * B : (r + 1) * B]
         return carry
 
-    lax.fori_loop(0, NB, cells_q, 0)
+    lax.fori_loop(0, NB, cells_q, 0, unroll=True)
 
     for c in scatter:
         c.wait_recv()
@@ -454,7 +469,7 @@
         S.l32[pl.ds(r, D, stride=H), :] = inv * (g - x * (inv * inv * inner))
         return carry
 
-    lax.fori_loop(0, H, last_norm, 0)
+    lax.fori_loop(0, H, last_norm, 0, unroll=True)
 
     def store(i, carry):
         x = S.l32[pl.ds(pl.multiple_of(i * step * H, step * H), step * H), :]

time: 62.5 us -> 53.4 us (0.85)
  Pallas kernels: 57.9 us -> 48.8 us
    pallas_call x1, Pallas kernels: 57.9 us -> 48.8 us  [per_device(): pl.pallas_call(functools.partial(kernel, nr, nc, names), out_shape=(jax.S...]
where the time goes in v2:
time: 53.4 us; the launch traced here: 53.2 us
  Pallas kernels  48.8 us (91%)
  local copies, waits for them, and re-layouts  3.74 us (7%)
  between operations  0.65 us (1%)
    pallas_call x1, Pallas kernels, per_device(): pl.pallas_call(functools.partial(kernel, nr, nc, names), out_shape=(jax.S...  48.8 us
    unnamed x7, local copies, waits for them, and re-layouts  3.74 us

profile of v2, /device:TPU:1, one launch (start us, length us, event | category | flops | bytes accessed | tf_op | source)
XLA Modules:
  0.0 53.2 jit_solution(8577542156062512307)
XLA Ops:
  0.6 48.8 %shard_map.85 = (bf16[256,8,128]{2,1,0:T(8,128)(2,1)}, f32[768,256]{1,0:T(8,128)}, f32[256,256]{1,0:T(8,128)}) custom-call(bf16[256,8,128]{2,1,0:T(8,128)(2,1)} %refs_0_.1, f32[1,256]{1,0:T(1,128)} %bitcast.1, bf16[768,256]{1,0:T(8,128)(2,1)} %refs_2_.1, bf16[256,256]{1,0:T(8,128)(2,1)} %refs_3_.1, f32[4]{0:T(128)} %refs_4_.1, bf16[256,8,128]{2,1,0:T(8,128)(2,1)} %refs_5_.1), custom_call_target="tpu_custom_call" | custom-call | tf_op jit(solution)/shard_map/pallas_call | solution.py:500
  49.5 0.0 copy-start
  49.5 1.9 %copy.12 = bf16[256,8,128]{2,1,0:T(8,128)(2,1)} copy(bf16[256,8,128]{2,1,0:T(8,128)(2,1)} %get-tuple-element.6) | data formatting | bytes 1048576
  51.4 0.0 copy-done
  51.4 0.0 copy-start.1
  51.4 0.9 %copy.13 = f32[768,256]{1,0:T(8,128)} copy(f32[768,256]{1,0:T(8,128)S(1)} %copy-done) | data formatting | bytes 1572864
  52.3 0.2 copy-done.1
  52.5 0.7 %copy.14 = f32[256,256]{1,0:T(8,128)} copy(f32[256,256]{1,0:T(8,128)S(1)} %copy-done.1) | data formatting | bytes 524288
Async XLA Ops:
  49.5 2.0 %copy-start = (f32[768,256]{1,0:T(8,128)S(1)}, f32[768,256]{1,0:T(8,128)}, u32[]{:S(2)}) copy-start(f32[768,256]{1,0:T(8,128)} %get-tuple-element.7) | copy-start | bytes 2359300
  51.4 1.1 %copy-start.1 = (f32[256,256]{1,0:T(8,128)S(1)}, f32[256,256]{1,0:T(8,128)}, u32[]{:S(2)}) copy-start(f32[256,256]{1,0:T(8,128)} %get-tuple-element.8) | copy-start | bytes 786436

commit v3 on v2

v3 whole, which is shorter than its diff:
```python
import collections
import functools
import math

import jax
import jax.numpy as jnp
from jax import lax
from jax.experimental import pallas as pl
from jax.experimental.pallas import tpu as pltpu
from jax.sharding import PartitionSpec as P

MESH = pl.DeviceIdType.MESH
F32 = jnp.float32
BF16 = jnp.bfloat16

D = 256
HEADS = 4
HW = 64
PW = 2 * HW
RADIUS = 3
EPS = 1e-06
H = 8
W = 128
B = 16
NB = W // B
QC = H * B
NG = NB + 1
ER = 16
ABOVE, BELOW, UNUSED = H, H + RADIUS, H + 2 * RADIUS
GC = ER * B
CHUNK = 64
WP = 4 * PW
HALF = WP // 2

DIRS = ((-1, 0), (1, 0), (0, -1), (0, 1), (-1, -1), (-1, 1), (1, -1), (1, 1))


def dot(a, b):
    return lax.dot_general(a, b, (((1,), (0,)), ((), ())), preferred_element_type=F32)


def dot_nt(a, b):
    return lax.dot_general(a, b, (((1,), (1,)), ((), ())), preferred_element_type=F32)


def heads(x):
    return x.reshape(x.shape[0] // HW, HW, x.shape[-1])


def flat(x):
    return x.reshape(x.shape[0] * HW, x.shape[-1])


def span(i, size):
    return slice(i * size, (i + 1) * size)


def at(i, size):
    return pl.ds(pl.multiple_of(i * size, size), size)


def norm_back(raw, inv, grad):
    inner = jnp.mean(grad * raw, axis=1, keepdims=True)
    return inv * (grad - raw * (inv * inv * inner))


def scratch_shapes(nr, nc):
    cc = HALF // nc
    ny = nr // 2
    dma = pltpu.SemaphoreType.DMA
    return collections.OrderedDict(
        lat=pltpu.VMEM((D, H, W), BF16),
        go=pltpu.VMEM((D, H, W), BF16),
        gain=pltpu.VMEM((1, D), F32),
        wqkv=pltpu.VMEM((3 * D, D), BF16),
        wo=pltpu.VMEM((D, D), BF16),
        gl=pltpu.VMEM((D, H, W), BF16),
        l32=pltpu.VMEM((D * H, W), F32),
        g32=pltpu.VMEM((D * H, W), F32),
        inv=pltpu.VMEM((H, W), F32),
        xr=pltpu.VMEM((H * W, D), BF16),
        xe32=pltpu.VMEM((2, H * 8, D), F32),
        xe=pltpu.VMEM((2, H * 8, D), BF16),
        rx_row=pltpu.VMEM((2, RADIUS * W, D), BF16),
        rx_col=pltpu.VMEM((2, H * 8, D), BF16),
        rx_cor=pltpu.VMEM((4, 32, D), BF16),
        xg=pltpu.VMEM((NG * GC, D), BF16),
        xb=pltpu.VMEM((NB * QC, D), BF16),
        gob=pltpu.VMEM((NB * QC, D), BF16),
        wot=pltpu.VMEM((D, D), BF16),
        wtq=pltpu.VMEM((D, D), BF16),
        wtp=pltpu.VMEM((2, D, 2 * PW), BF16),
        kraw=pltpu.VMEM((NG, D, GC), F32),
        kinv=pltpu.VMEM((NG, HEADS, 1, GC), F32),
        kc=pltpu.VMEM((NG, GC, D), BF16),
        vc=pltpu.VMEM((NG, GC, D), BF16),
        kt=pltpu.VMEM((NG, D, GC), BF16),
        vt=pltpu.VMEM((NG, D, GC), BF16),
        qraw=pltpu.VMEM((NB, D, QC), F32),
        qinv=pltpu.VMEM((NB, HEADS, 1, QC), F32),
        qm=pltpu.VMEM((NB, 2, PW, 2 * QC), BF16),
        gm=pltpu.VMEM((NB, 2, PW, 2 * QC), BF16),
        mask=pltpu.VMEM((3, 2 * GC, QC), F32),
        eb=pltpu.VMEM((2, 2 * GC, 2 * QC), BF16),
        sb=pltpu.VMEM((2, 2 * GC, 2 * QC), BF16),
        gk=pltpu.VMEM((PW, GC), F32),
        gv=pltpu.VMEM((PW, GC), F32),
        att=pltpu.VMEM((2, PW, NB * QC), BF16),
        gqb=pltpu.VMEM((2, PW, NB * QC), BF16),
        gkv=pltpu.VMEM((2, 2 * PW, NG * GC), BF16),
        gn=pltpu.VMEM((UNUSED, NG * B, D), F32),
        tx_row=pltpu.VMEM((2, RADIUS * W, D), BF16),
        tx_col=pltpu.VMEM((2, H * 8, D), BF16),
        tx_cor=pltpu.VMEM((4, 32, D), BF16),
        ry_row=pltpu.VMEM((2, RADIUS * W, D), BF16),
        ry_col=pltpu.VMEM((2, H * 8, D), BF16),
        ry_cor=pltpu.VMEM((4, 32, D), BF16),
        wg=pltpu.VMEM((2, WP, D), F32),
        wb=pltpu.VMEM((2, WP, D), BF16),
        rx_half=pltpu.VMEM((2, HALF, D), BF16),
        half=pltpu.VMEM((2, HALF, D), F32),
        hb=pltpu.VMEM((2, HALF, D), BF16),
        rx_pl=pltpu.VMEM((2, nc, cc, D), BF16),
        ys=pltpu.VMEM((2, ny, cc, D), F32),
        fb=pltpu.VMEM((2, HALF, D), BF16),
        cos=pltpu.SMEM((HEADS,), F32),
        s_in=dma((6,)),
        s_out=dma((3,)),
        s_hal=dma((8,)),
        r_hal=dma((8,)),
        s_ret=dma((8,)),
        r_ret=dma((8,)),
        s_core=dma((2, 2)),
        r_core=dma((2, 2)),
        s_pl=dma((2, 2, nc)),
        r_pl=dma((2, 2, nc)),
        s_y=dma((2, ny)),
        r_y=dma((2, ny)),
    )


def kernel(nr, nc, names, *refs):
    S = collections.namedtuple("S", names)(*refs)
    row, col = lax.axis_index("row"), lax.axis_index("col")
    core, ypos = lax.rem(row, 2), lax.div(row, 2)
    ny = nr // 2
    cc = HALF // nc

    def there(dr, dc):
        return (lax.rem(row + (dr % nr), nr), lax.rem(col + (dc % nc), nc))

    mate = (row + 1 - 2 * core, col)
    sent = []

    def remote(src, dst, send, recv, device):
        return pltpu.make_async_remote_copy(
            src_ref=src, dst_ref=dst, send_sem=send, recv_sem=recv, device_id=device, device_id_type=MESH
        )

    def send(*args):
        copy = remote(*args)
        copy.start()
        sent.append(copy)
        return copy

    partners = list(DIRS)
    partners += [(0, k) for k in range(2, nc - 1)]
    partners += [(2 * m, 0) for m in range(1, ny)]
    barrier = pltpu.get_barrier_semaphore()
    for dr, dc in partners:
        pl.semaphore_signal(barrier, inc=1, device_id=there(dr, dc), device_id_type=MESH)
    loads = []
    for i, (src, dst) in enumerate(
        ((S.h_lat, S.lat), (S.h_gain, S.gain), (S.h_go, S.go), (S.h_wqkv, S.wqkv), (S.h_wo, S.wo), (S.h_cos, S.cos))
    ):
        loads.append(pltpu.make_async_copy(src, dst, S.s_in.at[i]))
        loads[-1].start()

    step = 32

    def load(i, acc):
        x = S.lat[pl.ds(i * step, step)].astype(F32)
        S.l32[at(i, step * H), :] = x.reshape(step * H, W)
        return acc + jnp.sum(x * x, axis=0)

    loads[0].wait()
    total = lax.fori_loop(0, D // step, load, jnp.zeros((H, W), F32))
    S.inv[...] = lax.rsqrt(total * (1.0 / D) + EPS)
    loads[1].wait()
    gain = S.gain[...]

    for r in range(H):
        x = S.l32[pl.ds(r, D, stride=H), :] * S.inv[r : r + 1, :]
        xn = x.T * gain
        xnb = xn.astype(BF16)
        S.xr[span(r, W), :] = xnb
        S.xe32[0, span(r, 8), :] = xn[:8]
        S.xe32[1, span(r, 8), :] = xn[W - 8 :]
        for j in range(NB):
            S.xb[span(j * H + r, B), :] = xnb[span(j, B)]
        for g in range(1, NB):
            S.xg[span(g * ER + r, B), :] = xn[g * B - 8 : g * B + 8].astype(BF16)
    S.xe[...] = S.xe32[...].astype(BF16)

    pl.semaphore_wait(barrier, len(partners))
    near = RADIUS * W
    edge = {-1: slice(0, near), 1: slice(H * W - near, H * W)}
    part = {-1: slice(0, 32), 1: slice(32, 64)}
    halo = []
    for i, (dr, dc) in enumerate(DIRS):
        if dc == 0:
            src, dst = S.xr.at[edge[dr]], S.rx_row.at[i]
        elif dr == 0:
            src, dst = S.xe.at[(dc + 1) // 2], S.rx_col.at[i - 2]
        else:
            src, dst = S.xe.at[(dc + 1) // 2, part[dr]], S.rx_cor.at[i - 4]
        halo.append(send(src, dst, S.s_hal.at[i], S.r_hal.at[i], there(dr, dc)))

    for c in loads[2:]:
        c.wait()
    S.wot[...] = S.wo[...].T
    S.wtq[...] = S.wqkv[0:D, :].T
    for p in range(2):
        for i in range(2):
            a = (1 + i) * D + p * PW
            S.wtp[p, :, span(i, PW)] = S.wqkv[a : a + PW, :].T

    def widen(i, carry):
        x = S.go[pl.ds(i * step, step)].astype(F32)
        S.g32[at(i, step * H), :] = x.reshape(step * H, W)
        return carry

    lax.fori_loop(0, D // step, widen, 0)
    for r in range(H):
        g = S.g32[pl.ds(r, D, stride=H), :].T.astype(BF16)
        for j in range(NB):
            S.gob[span(j * H + r, B), :] = g[span(j, B)]

    mshape = (2, ER, B, QC)
    half_, kr, kc = (lax.broadcasted_iota(jnp.int32, mshape, a) for a in range(3))
    lane = lax.broadcasted_iota(jnp.int32, mshape, 3)
    qr, qc = lax.div(lane, B), lax.rem(lane, B)
    krow = jnp.where(kr < ABOVE, kr, jnp.where(kr < BELOW, kr - ABOVE - RADIUS, kr - BELOW + H))
    dr = krow - qr
    off = B * half_ + kc - 8
    dc = off - qc
    grow = row * H + krow
    ok = (dr >= -RADIUS) & (dr <= RADIUS) & (dc >= -RADIUS) & (dc <= RADIUS)
    ok = ok & (grow >= 0) & (grow < nr * H) & (kr < UNUSED)
    one = jnp.where(ok, 1.0, 0.0).astype(F32).reshape(2 * GC, QC)
    off = off.reshape(2 * GC, QC)
    S.mask[0] = jnp.where(col * W + off >= 0, one, 0.0)
    S.mask[1] = one
    S.mask[2] = jnp.where(col * W + W - B + off < nc * W, one, 0.0)

    zero = jnp.zeros((HW, QC), BF16)
    for j in range(NB):
        q = heads(dot_nt(S.wqkv[0:D, :], S.xb[span(j, QC), :]))
        inv = lax.rsqrt(jnp.mean(q * q, axis=1, keepdims=True) + EPS)
        qn = (q * inv).astype(BF16)
        S.qraw[j] = flat(q)
        S.qinv[j] = inv
        ga = heads(dot_nt(S.wot[...], S.gob[span(j, QC), :])).astype(BF16)
        for p in range(2):
            for x, out in ((qn, S.qm), (ga, S.gm)):
                out[j, p, 0:HW, :] = jnp.concatenate([x[2 * p], zero], axis=1)
                out[j, p, HW:PW, :] = jnp.concatenate([zero, x[2 * p + 1]], axis=1)

    def pairs(*units):
        x = jnp.concatenate([S.xg[span(2 * g + s, GC // 2), :] for g, s in units], axis=0)
        kv = dot_nt(S.wqkv[D : 3 * D, :], x)
        k = heads(kv[:D])
        inv = lax.rsqrt(jnp.mean(k * k, axis=1, keepdims=True) + EPS)
        kn = flat(k * inv).astype(BF16)
        v = kv[D:].astype(BF16)
        knt, vnt = kn.T, v.T
        for n, (g, s) in enumerate(units):
            here, lanes = span(s, GC // 2), span(n, GC // 2)
            S.kraw[g, :, here] = kv[:D, lanes]
            S.kinv[g, :, :, here] = inv[:, :, lanes]
            S.kt[g, :, here] = kn[:, lanes]
            S.vt[g, :, here] = v[:, lanes]
            S.kc[g, here, :] = knt[lanes]
            S.vc[g, here, :] = vnt[lanes]

    for g in range(1, NB - 1, 2):
        pairs((g, 0), (g + 1, 0))

    for c in halo:
        c.wait_recv()
    left = S.rx_col[1].astype(F32)
    right = S.rx_col[0].astype(F32)

    def ends(er, first, last, l8, r8):
        S.xg[span(er, B), :] = jnp.concatenate([l8, first], axis=0).astype(BF16)
        S.xg[span(NB * ER + er, B), :] = jnp.concatenate([last, r8], axis=0).astype(BF16)

    for r in range(H):
        ends(r, S.xe32[0, span(r, 8), :], S.xe32[1, span(r, 8), :], left[span(r, 8)], right[span(r, 8)])
    for down in (0, 1):
        l_cor = S.rx_cor[2 * down + 1].astype(F32)
        r_cor = S.rx_cor[2 * down].astype(F32)
        for i in range(RADIUS):
            er = (ABOVE if down else BELOW) + i
            n = i + 1 if down else i
            line = S.rx_row[down, span(i, W), :].astype(F32)
            for g in range(1, NB):
                S.xg[span(g * ER + er, B), :] = line[g * B - 8 : g * B + 8].astype(BF16)
            ends(er, line[:8], line[-8:], l_cor[span(n, 8)], r_cor[span(n, 8)])
    for g in range(NG):
        S.xg[g * GC + UNUSED * B : (g + 1) * GC, :] = jnp.zeros((2 * B, D), BF16)
    units = [(NB - 1, 0), (0, 0), (NB, 0)] + [(g, 1) for g in range(NG)]
    for n in range(0, len(units), 2):
        pairs(*units[n : n + 2])

    factor = [S.cos[h] * (1.0 / HW) for h in range(HEADS)]

    def by_lane(values):
        return jnp.concatenate([jnp.full((1, QC), x, F32) for x in values], axis=1)

    def key_done(p, g, gk, gv):
        o = span(p, PW)
        gk = jnp.concatenate([gk[span(i, HW)] * factor[2 * p + i] for i in range(2)], axis=0)
        gk = norm_back(heads(S.kraw[g, o, :]), S.kinv[g, 2 * p : 2 * p + 2], heads(gk))
        S.gkv[p, 0:PW, at(g, GC)] = flat(gk).astype(BF16)
        S.gkv[p, PW : 2 * PW, at(g, GC)] = gv.astype(BF16)

    def attention(p, n, carry):
        o = span(p, PW)
        far = by_lane(factor[2 * p : 2 * p + 2])
        lgr = far * math.log2(math.e)
        first = []
        for t in range(2):
            j = 2 * n + t
            keys = jnp.concatenate([S.kc[j, :, o], S.kc[j + 1, :, o]], axis=0)
            vals = jnp.concatenate([S.vc[j, :, o], S.vc[j + 1, :, o]], axis=0)
            first.append((dot(keys, S.qm[j, p]), dot(vals, S.gm[j, p])))
        for t in range(2):
            j = 2 * n + t
            which = jnp.where(j == 0, 0, jnp.where(j == NB - 1, 2, 1))
            score, prod = first[t]
            tot = jnp.zeros((8, 2 * QC), F32)
            ed = jnp.zeros((8, 2 * QC), F32)
            for c in range(0, 2 * GC, CHUNK):
                mk = S.mask[which, c : c + CHUNK, :]
                e = jnp.exp2(score[c : c + CHUNK] * lgr) * jnp.concatenate([mk, mk], axis=1)
                tot = tot + jnp.sum(e.reshape(CHUNK // 8, 8, 2 * QC), axis=0)
                ed = ed + jnp.sum((e * prod[c : c + CHUNK]).reshape(CHUNK // 8, 8, 2 * QC), axis=0)
                S.eb[t, c : c + CHUNK, :] = e.astype(BF16)
            rt = 1.0 / jnp.sum(tot, axis=0, keepdims=True)
            mean = jnp.sum(ed, axis=0, keepdims=True) * rt
            for c in range(0, 2 * GC, CHUNK):
                e = S.eb[t, c : c + CHUNK, :].astype(F32)
                S.sb[t, c : c + CHUNK, :] = (e * (prod[c : c + CHUNK] - mean)).astype(BF16)
            prob = S.eb[t]
            slope = S.sb[t]
            keys_t = jnp.concatenate([S.kt[j, o, :], S.kt[j + 1, o, :]], axis=1)
            vals_t = jnp.concatenate([S.vt[j, o, :], S.vt[j + 1, o, :]], axis=1)
            attn = dot(vals_t, prob) * rt
            grad_q = dot(keys_t, slope) * (rt * far)
            for i in range(2):
                c, lanes = span(i, HW), span(i, QC)
                S.att[p, c, at(j, QC)] = attn[c, lanes].astype(BF16)
                raw = S.qraw[j, span(2 * p + i, HW), :]
                g = norm_back(heads(raw), S.qinv[j, 2 * p + i : 2 * p + i + 1], heads(grad_q[c, lanes]))
                S.gqb[p, c, at(j, QC)] = flat(g).astype(BF16)
            qs = (S.qm[j, p].astype(F32) * rt).astype(BF16)
            gs = (S.gm[j, p].astype(F32) * rt).astype(BF16)
            grad_k = dot_nt(qs, slope)
            grad_v = dot_nt(gs, prob)
            key_done(p, j, S.gk[...] + grad_k[:, :GC], S.gv[...] + grad_v[:, :GC])
            S.gk[...] = grad_k[:, GC:]
            S.gv[...] = grad_v[:, GC:]
        return carry

    def begin():
        S.gk[...] = jnp.zeros((PW, GC), F32)
        S.gv[...] = jnp.zeros((PW, GC), F32)

    def weights(p):
        key_done(p, NB, S.gk[...], S.gv[...])
        S.wg[p, 0:PW, :] = dot(S.gqb[p], S.xb[...])
        S.wg[p, PW : 3 * PW, :] = dot(S.gkv[p], S.xg[...])
        S.wg[p, 3 * PW :, :] = dot(S.att[p], S.gob[...])
        S.wb[p] = S.wg[p].astype(BF16)

    mine = at(core, HALF)

    def to_core(p):
        return [send(S.wb.at[p, at(1 - core, HALF)], S.rx_half.at[p], S.s_core.at[p, 0], S.r_core.at[p, 0], mate)]

    def to_row(p):
        half = S.wg[p, mine, :] + S.rx_half[p].astype(F32)
        S.half[p] = half
        S.hb[p] = half.astype(BF16)
        out = []
        for k in range(1, nc):
            t = lax.rem(col + k, nc)
            out.append(send(S.hb.at[p, at(t, cc)], S.rx_pl.at[p, k], S.s_pl.at[p, 0, k], S.r_pl.at[p, 0, k], (row, t)))
        return out

    def to_y(p):
        chunk = S.half[p, at(col, cc), :]
        for k in range(1, nc):
            chunk = chunk + S.rx_pl[p, k].astype(F32)
        S.ys[p, ypos] = chunk
        slot = S.ys.at[p, ypos]
        return [send(slot, slot, S.s_y.at[p, m], S.r_y.at[p, m], there(2 * m, 0)) for m in range(1, ny)]

    def back_to_row(p):
        chunk = S.ys[p, 0]
        for m in range(1, ny):
            chunk = chunk + S.ys[p, m]
        S.fb[p, at(col, cc), :] = (chunk * (1.0 / math.sqrt(nr * H * nc * W))).astype(BF16)
        slot = S.fb.at[p, at(col, cc)]
        return [send(slot, slot, S.s_pl.at[p, 1, k], S.r_pl.at[p, 1, k], there(0, k)) for k in range(1, nc)]

    stores = []

    def back_to_core(p):
        stores.append(pltpu.make_async_copy(S.fb.at[p], S.h_gw.at[p, mine], S.s_out.at[p]))
        stores[-1].start()
        return [send(S.fb.at[p], S.h_gw.at[p, mine], S.s_core.at[p, 1], S.r_core.at[p, 1], mate)]

    def arrived(copies):
        for c in copies:
            c.wait_recv()

    begin()
    lax.fori_loop(0, NB // 2, functools.partial(attention, 0), 0)
    weights(0)
    core0 = to_core(0)

    begin()
    lax.fori_loop(0, NB // 4, functools.partial(attention, 1), 0)
    arrived(core0)
    row0 = to_row(0)
    lax.fori_loop(NB // 4, NB // 2, functools.partial(attention, 1), 0)
    weights(1)
    core1 = to_core(1)

    def cells_kv(g):
        x = sum(dot(S.wtp[p], S.gkv[p, :, span(g, GC)]) for p in range(2)).T
        for er in range(UNUSED):
            S.gn[er, span(g, B), :] = x[span(er, B)]

    for g in range(4):
        cells_kv(g)
    arrived(core1)
    row1 = to_row(1)
    for g in range(4, NG):
        cells_kv(g)

    low, high = 8, 8 + W
    rows_at = {-1: slice(ABOVE, BELOW), 1: slice(BELOW, UNUSED)}
    cols_at = {-1: slice(0, 8), 1: slice(high, high + 8)}
    back = []
    for i, (dr, dc) in enumerate(DIRS):
        if dc == 0:
            S.tx_row[i] = S.gn[rows_at[dr], low:high, :].reshape(RADIUS * W, D).astype(BF16)
            src, dst = S.tx_row.at[i], S.ry_row.at[i]
        elif dr == 0:
            S.tx_col[i - 2] = S.gn[0:H, cols_at[dc], :].reshape(H * 8, D).astype(BF16)
            src, dst = S.tx_col.at[i - 2], S.ry_col.at[i - 2]
        else:
            cor = S.gn[rows_at[dr], cols_at[dc], :].reshape(RADIUS * 8, D)
            S.tx_cor[i - 4] = jnp.concatenate([cor, jnp.zeros((8, D), F32)], axis=0).astype(BF16)
            src, dst = S.tx_cor.at[i - 4], S.ry_cor.at[i - 4]
        back.append(send(src, dst, S.s_ret.at[i], S.r_ret.at[i], there(dr, dc)))
    arrived(row0)
    y0 = to_y(0)

    for j in range(NB):
        g = jnp.concatenate([S.gqb[p, :, span(j, QC)] for p in range(2)], axis=0)
        x = dot(S.wtq[...], g).T
        for r in range(H):
            S.gn[r, j * B + 8 : j * B + 8 + B, :] += x[span(r, B)]
    arrived(row1)
    y1 = to_y(1)

    arrived(y0)
    gather0 = back_to_row(0)
    arrived(back)
    last = H - RADIUS
    S.gn[last:H, low:high, :] += S.ry_row[0].astype(F32).reshape(RADIUS, W, D)
    S.gn[0:RADIUS, low:high, :] += S.ry_row[1].astype(F32).reshape(RADIUS, W, D)
    S.gn[0:H, high - 8 : high, :] += S.ry_col[0].astype(F32).reshape(H, 8, D)
    S.gn[0:H, low : low + 8, :] += S.ry_col[1].astype(F32).reshape(H, 8, D)
    for i, (dr, dc) in enumerate(DIRS[4:]):
        a = last if dr == -1 else 0
        b = high - 8 if dc == -1 else low
        cor = S.ry_cor[i].astype(F32)[: RADIUS * 8]
        S.gn[a : a + RADIUS, b : b + 8, :] += cor.reshape(RADIUS, 8, D)
    arrived(y1)
    gather1 = back_to_row(1)

    for r in range(H):
        g = (S.gn[r, low:high, :] * gain).T
        x = S.l32[pl.ds(r, D, stride=H), :]
        inv = S.inv[r : r + 1, :]
        inner = jnp.mean(g * x, axis=0, keepdims=True)
        S.l32[pl.ds(r, D, stride=H), :] = inv * (g - x * (inv * inv * inner))

    def store(i, carry):
        S.gl[pl.ds(i * step, step)] = S.l32[at(i, step * H), :].reshape(step, H, W).astype(BF16)
        return carry

    lax.fori_loop(0, D // step, store, 0)
    stores.append(pltpu.make_async_copy(S.gl, S.h_gl, S.s_out.at[2]))
    stores[-1].start()

    arrived(gather0)
    done0 = back_to_core(0)
    arrived(gather1)
    done1 = back_to_core(1)
    arrived(done0)
    arrived(done1)
    for c in stores:
        c.wait()
    for c in sent:
        c.wait_send()


def finish(gl, gw, out, gwqkv, gwo):
    out[...] = gl[...]
    for p in range(2):
        for i in range(3):
            gwqkv[i * D + p * PW : i * D + (p + 1) * PW, :] = gw[p, span(i, PW), :].astype(F32)
        gwo[:, span(p, PW)] = gw[p, 3 * PW :, :].astype(F32).T


def solution(mesh):
    nr, nc = mesh.shape["row"], mesh.shape["col"]
    scratch = scratch_shapes(nr, nc)
    names = ["h_lat", "h_gain", "h_wqkv", "h_wo", "h_cos", "h_go", "h_gl", "h_gw", *scratch]
    hbm = pl.BlockSpec(memory_space=pl.ANY)
    vmem = pl.BlockSpec(memory_space=pltpu.VMEM)

    def per_device(latent, norm_gain, qkv_weight, out_weight, cos_scale, grad_output):
        gl, gw = pl.pallas_call(
            functools.partial(kernel, nr, nc, names),
            out_shape=(jax.ShapeDtypeStruct((D, H, W), BF16), jax.ShapeDtypeStruct((2, WP, D), BF16)),
            in_specs=[hbm] * 6,
            out_specs=(hbm, hbm),
            scratch_shapes=list(scratch.values()),
            compiler_params=pltpu.CompilerParams(
                collective_id=0, has_side_effects=True, vmem_limit_bytes=60 * 2**20
            ),
        )(latent, norm_gain.reshape(1, D), qkv_weight, out_weight, cos_scale, grad_output)
        return pl.pallas_call(
            finish,
            out_shape=(
                jax.ShapeDtypeStruct((D, H, W), BF16),
                jax.ShapeDtypeStruct((3 * D, D), F32),
                jax.ShapeDtypeStruct((D, D), F32),
            ),
            in_specs=[vmem, vmem],
            out_specs=(vmem, vmem, vmem),
                    )(gl, gw)

    return jax.shard_map(
        per_device,
        mesh=mesh,
        in_specs=(P(None, "row", "col"), P(), P(), P(), P(), P(None, "row", "col")),
        out_specs=(P(None, "row", "col"), P(), P()),
        check_vma=False,
    )
```

time: 53.4 us -> 47.1 us (0.88)
  local copies, waits for them, and re-layouts: 3.74 us -> 0 us
  Pallas kernels: 48.8 us -> 46.3 us
    pallas_call x1, Pallas kernels: 48.8 us -> 43.9 us  [per_device(): pl.pallas_call(functools.partial(kernel, nr, nc, names), out_shape=(jax.S...]
    unnamed x7 -> x0, local copies, waits for them, and re-layouts: 3.74 us -> none
    pallas_call x0 -> x1, Pallas kernels: none -> 2.41 us  [per_device(): pl.pallas_call(finish, out_shape=(jax.ShapeDtypeStruct((D, H, W), BF16),...]
where the time goes in v3:
time: 47.1 us; the launch traced here: 46.9 us
  Pallas kernels  46.3 us (98%)
  between operations  0.64 us (1%)
    pallas_call x1, Pallas kernels, per_device(): pl.pallas_call(functools.partial(kernel, nr, nc, names), out_shape=(jax.S...  43.9 us
    pallas_call x1, Pallas kernels, per_device(): pl.pallas_call(finish, out_shape=(jax.ShapeDtypeStruct((D, H, W), BF16),...  2.41 us

profile of v3, /device:TPU:1, one launch (start us, length us, event | category | flops | bytes accessed | tf_op | source)
XLA Modules:
  0.0 46.9 jit_solution(2278536334306807781)
XLA Ops:
  0.6 43.9 %shard_map.85 = (bf16[256,8,128]{2,1,0:T(8,128)(2,1)}, bf16[2,512,256]{2,1,0:T(8,128)(2,1)}) custom-call(bf16[256,8,128]{2,1,0:T(8,128)(2,1)} %refs_0_.1, f32[1,256]{1,0:T(1,128)} %bitcast.1, bf16[768,256]{1,0:T(8,128)(2,1)} %refs_2_.1, bf16[256,256]{1,0:T(8,128)(2,1)} %refs_3_.1, f32[4]{0:T(128)} %refs_4_.1, bf16[256,8,128]{2,1,0:T(8,128)(2,1)} %refs_5_.1), custom_call_target="tpu_custom_call" | custom-call | tf_op jit(solution)/shard_map/pallas_call | solution.py:540
  44.5 2.4 %shard_map.86 = (bf16[256,8,128]{2,1,0:T(8,128)(2,1)}, f32[768,256]{1,0:T(8,128)}, f32[256,256]{1,0:T(8,128)}) custom-call(bf16[256,8,128]{2,1,0:T(8,128)(2,1)} %get-tuple-element.5.gl, bf16[2,512,256]{2,1,0:T(8,128)(2,1)} %get-tuple-element.6.gw), custom_call_target="tpu_custom_call" | custom-call | tf_op jit(solution)/shard_map/pallas_call | solution.py:550

commit v4 on v3

--- a/solution.py
+++ b/solution.py
@@ -74,7 +74,6 @@
         gain=pltpu.VMEM((1, D), F32),
         wqkv=pltpu.VMEM((3 * D, D), BF16),
         wo=pltpu.VMEM((D, D), BF16),
-        gl=pltpu.VMEM((D, H, W), BF16),
         l32=pltpu.VMEM((D * H, W), F32),
         g32=pltpu.VMEM((D * H, W), F32),
         inv=pltpu.VMEM((H, W), F32),
@@ -122,10 +121,8 @@
         hb=pltpu.VMEM((2, HALF, D), BF16),
         rx_pl=pltpu.VMEM((2, nc, cc, D), BF16),
         ys=pltpu.VMEM((2, ny, cc, D), F32),
-        fb=pltpu.VMEM((2, HALF, D), BF16),
         cos=pltpu.SMEM((HEADS,), F32),
         s_in=dma((6,)),
-        s_out=dma((3,)),
         s_hal=dma((8,)),
         r_hal=dma((8,)),
         s_ret=dma((8,)),
@@ -411,16 +408,14 @@
         chunk = S.ys[p, 0]
         for m in range(1, ny):
             chunk = chunk + S.ys[p, m]
-        S.fb[p, at(col, cc), :] = (chunk * (1.0 / math.sqrt(nr * H * nc * W))).astype(BF16)
-        slot = S.fb.at[p, at(col, cc)]
+        place = pl.ds(pl.multiple_of(core * HALF + col * cc, cc), cc)
+        S.gw[p, place, :] = (chunk * (1.0 / math.sqrt(nr * H * nc * W))).astype(BF16)
+        slot = S.gw.at[p, place]
         return [send(slot, slot, S.s_pl.at[p, 1, k], S.r_pl.at[p, 1, k], there(0, k)) for k in range(1, nc)]
 
-    stores = []
-
     def back_to_core(p):
-        stores.append(pltpu.make_async_copy(S.fb.at[p], S.h_gw.at[p, mine], S.s_out.at[p]))
-        stores[-1].start()
-        return [send(S.fb.at[p], S.h_gw.at[p, mine], S.s_core.at[p, 1], S.r_core.at[p, 1], mate)]
+        slot = S.gw.at[p, mine]
+        return [send(slot, slot, S.s_core.at[p, 1], S.r_core.at[p, 1], mate)]
 
     def arrived(copies):
         for c in copies:
@@ -506,8 +501,6 @@
         return carry
 
     lax.fori_loop(0, D // step, store, 0)
-    stores.append(pltpu.make_async_copy(S.gl, S.h_gl, S.s_out.at[2]))
-    stores[-1].start()
 
     arrived(gather0)
     done0 = back_to_core(0)
@@ -515,8 +508,6 @@
     done1 = back_to_core(1)
     arrived(done0)
     arrived(done1)
-    for c in stores:
-        c.wait()
     for c in sent:
         c.wait_send()
 
@@ -532,21 +523,26 @@
 def solution(mesh):
     nr, nc = mesh.shape["row"], mesh.shape["col"]
     scratch = scratch_shapes(nr, nc)
-    names = ["h_lat", "h_gain", "h_wqkv", "h_wo", "h_cos", "h_go", "h_gl", "h_gw", *scratch]
-    hbm = pl.BlockSpec(memory_space=pl.ANY)
+    names = ["h_lat", "h_gain", "h_wqkv", "h_wo", "h_cos", "h_go", "gl", "gw", *scratch]
+    hbm = pl.BlockSpec(memory_space=pltpu.HBM)
     vmem = pl.BlockSpec(memory_space=pltpu.VMEM)
 
     def per_device(latent, norm_gain, qkv_weight, out_weight, cos_scale, grad_output):
         gl, gw = pl.pallas_call(
             functools.partial(kernel, nr, nc, names),
-            out_shape=(jax.ShapeDtypeStruct((D, H, W), BF16), jax.ShapeDtypeStruct((2, WP, D), BF16)),
+            out_shape=(pltpu.VMEM((D, H, W), BF16), pltpu.VMEM((2, WP, D), BF16)),
             in_specs=[hbm] * 6,
-            out_specs=(hbm, hbm),
+            out_specs=(vmem, vmem),
             scratch_shapes=list(scratch.values()),
             compiler_params=pltpu.CompilerParams(
-                collective_id=0, has_side_effects=True, vmem_limit_bytes=60 * 2**20
+                collective_id=0, has_side_effects=True, vmem_limit_bytes=44 * 2**20
             ),
-        )(latent, norm_gain.reshape(1, D), qkv_weight, out_weight, cos_scale, grad_output)
+        )(
+            *(
+                pltpu.with_memory_space_constraint(x, pltpu.HBM)
+                for x in (latent, norm_gain.reshape(1, D), qkv_weight, out_weight, cos_scale, grad_output)
+            )
+        )
         return pl.pallas_call(
             finish,
             out_shape=(
@@ -556,7 +552,8 @@
             ),
             in_specs=[vmem, vmem],
             out_specs=(vmem, vmem, vmem),
-                    )(gl, gw)
+                        compiler_params=pltpu.CompilerParams(vmem_limit_bytes=16 * 2**20),
+        )(*(pltpu.with_memory_space_constraint(x, pltpu.VMEM) for x in (gl, gw)))
 
     return jax.shard_map(
         per_device,

time: 47.1 us -> 45.7 us (0.970)
  Pallas kernels: 46.3 us -> 44.9 us
    pallas_call x1, Pallas kernels: 2.41 us -> 1.22 us  [per_device(): pl.pallas_call(finish, out_shape=(jax.ShapeDtypeStruct((D, H, W), BF16),...]
where the time goes in v4:
time: 45.7 us; the launch traced here: 45.6 us
  Pallas kernels  44.9 us (98%)
  between operations  0.64 us (1%)
    pallas_call x1, Pallas kernels, per_device(): pl.pallas_call(functools.partial(kernel, nr, nc, names), out_shape=(pltpu...  43.7 us
    pallas_call x1, Pallas kernels, per_device(): pl.pallas_call(finish, out_shape=(jax.ShapeDtypeStruct((D, H, W), BF16),...  1.22 us

profile of v4, /device:TPU:1, one launch (start us, length us, event | category | flops | bytes accessed | tf_op | source)
XLA Modules:
  0.0 45.6 jit_solution(11417091123691100689)
XLA Ops:
  0.6 43.7 %shard_map.85 = (bf16[256,8,128]{2,1,0:T(8,128)(2,1)S(1)}, bf16[2,512,256]{2,1,0:T(8,128)(2,1)S(1)}) custom-call(bf16[256,8,128]{2,1,0:T(8,128)(2,1)} %refs_0_.1, f32[1,256]{1,0:T(1,128)} %bitcast.1, bf16[768,256]{1,0:T(8,128)(2,1)} %refs_2_.1, bf16[256,256]{1,0:T(8,128)(2,1)} %refs_3_.1, f32[4]{0:T(128)} %refs_4_.1, bf16[256,8,128]{2,1,0:T(8,128)(2,1)} %refs_5_.1), custom_call_target="tpu_custom_call" | custom-call | tf_op jit(solution)/shard_map/pallas_call | solution.py:531
  44.4 1.2 %shard_map.86 = (bf16[256,8,128]{2,1,0:T(8,128)(2,1)}, f32[768,256]{1,0:T(8,128)}, f32[256,256]{1,0:T(8,128)}) custom-call(bf16[256,8,128]{2,1,0:T(8,128)(2,1)S(1)} %get-tuple-element.5.gl, bf16[2,512,256]{2,1,0:T(8,128)(2,1)S(1)} %get-tuple-element.6.gw), custom_call_target="tpu_custom_call" | custom-call | tf_op jit(solution)/shard_map/pallas_call | solution.py:546

commit v5 on v4

--- a/solution.py
+++ b/solution.py
@@ -129,8 +129,8 @@
         r_ret=dma((8,)),
         s_core=dma((2, 2)),
         r_core=dma((2, 2)),
-        s_pl=dma((2, 2, nc)),
-        r_pl=dma((2, 2, nc)),
+        s_pl=dma((2, 2)),
+        r_pl=dma((2, 2)),
         s_y=dma((2, ny)),
         r_y=dma((2, ny)),
     )
@@ -159,6 +159,11 @@
         copy.start()
         sent.append(copy)
         return copy
+
+    def departed():
+        for c in sent:
+            c.wait_send()
+        sent.clear()
 
     partners = list(DIRS)
     partners += [(0, k) for k in range(2, nc - 1)]
@@ -390,11 +395,13 @@
         half = S.wg[p, mine, :] + S.rx_half[p].astype(F32)
         S.half[p] = half
         S.hb[p] = half.astype(BF16)
-        out = []
         for k in range(1, nc):
             t = lax.rem(col + k, nc)
-            out.append(send(S.hb.at[p, at(t, cc)], S.rx_pl.at[p, k], S.s_pl.at[p, 0, k], S.r_pl.at[p, 0, k], (row, t)))
-        return out
+            remote(S.hb.at[p, at(t, cc)], S.rx_pl.at[p, k], S.s_pl.at[p, 0], S.r_pl.at[p, 0], (row, t)).start()
+
+    def whole_row(p, semaphore):
+        rows = S.rx_pl.at[p, 1:nc]
+        pltpu.make_async_copy(rows, rows, semaphore).wait()
 
     def to_y(p):
         chunk = S.half[p, at(col, cc), :]
@@ -411,7 +418,8 @@
         place = pl.ds(pl.multiple_of(core * HALF + col * cc, cc), cc)
         S.gw[p, place, :] = (chunk * (1.0 / math.sqrt(nr * H * nc * W))).astype(BF16)
         slot = S.gw.at[p, place]
-        return [send(slot, slot, S.s_pl.at[p, 1, k], S.r_pl.at[p, 1, k], there(0, k)) for k in range(1, nc)]
+        for k in range(1, nc):
+            remote(slot, slot, S.s_pl.at[p, 1], S.r_pl.at[p, 1], there(0, k)).start()
 
     def back_to_core(p):
         slot = S.gw.at[p, mine]
@@ -429,7 +437,7 @@
     begin()
     lax.fori_loop(0, NB // 4, functools.partial(attention, 1), 0)
     arrived(core0)
-    row0 = to_row(0)
+    to_row(0)
     lax.fori_loop(NB // 4, NB // 2, functools.partial(attention, 1), 0)
     weights(1)
     core1 = to_core(1)
@@ -442,7 +450,7 @@
     for g in range(4):
         cells_kv(g)
     arrived(core1)
-    row1 = to_row(1)
+    to_row(1)
     for g in range(4, NG):
         cells_kv(g)
 
@@ -462,7 +470,7 @@
             S.tx_cor[i - 4] = jnp.concatenate([cor, jnp.zeros((8, D), F32)], axis=0).astype(BF16)
             src, dst = S.tx_cor.at[i - 4], S.ry_cor.at[i - 4]
         back.append(send(src, dst, S.s_ret.at[i], S.r_ret.at[i], there(dr, dc)))
-    arrived(row0)
+    whole_row(0, S.r_pl.at[0, 0])
     y0 = to_y(0)
 
     for j in range(NB):
@@ -470,11 +478,11 @@
         x = dot(S.wtq[...], g).T
         for r in range(H):
             S.gn[r, j * B + 8 : j * B + 8 + B, :] += x[span(r, B)]
-    arrived(row1)
+    whole_row(1, S.r_pl.at[1, 0])
     y1 = to_y(1)
 
     arrived(y0)
-    gather0 = back_to_row(0)
+    back_to_row(0)
     arrived(back)
     last = H - RADIUS
     S.gn[last:H, low:high, :] += S.ry_row[0].astype(F32).reshape(RADIUS, W, D)
@@ -487,7 +495,7 @@
         cor = S.ry_cor[i].astype(F32)[: RADIUS * 8]
         S.gn[a : a + RADIUS, b : b + 8, :] += cor.reshape(RADIUS, 8, D)
     arrived(y1)
-    gather1 = back_to_row(1)
+    back_to_row(1)
 
     for r in range(H):
         g = (S.gn[r, low:high, :] * gain).T
@@ -502,14 +510,18 @@
 
     lax.fori_loop(0, D // step, store, 0)
 
-    arrived(gather0)
+    departed()
+    whole_row(0, S.s_pl.at[0, 0])
+    whole_row(1, S.s_pl.at[1, 0])
+    whole_row(0, S.s_pl.at[0, 1])
+    whole_row(0, S.r_pl.at[0, 1])
     done0 = back_to_core(0)
-    arrived(gather1)
+    whole_row(1, S.r_pl.at[1, 1])
     done1 = back_to_core(1)
     arrived(done0)
     arrived(done1)
-    for c in sent:
-        c.wait_send()
+    departed()
+    whole_row(1, S.s_pl.at[1, 1])
 
 
 def finish(gl, gw, out, gwqkv, gwo):

time: 45.7 us -> 44.5 us (0.974)
  Pallas kernels: 44.9 us -> 43.7 us
    pallas_call x1, Pallas kernels: 43.7 us -> 42.5 us  [per_device(): pl.pallas_call(functools.partial(kernel, nr, nc, names), out_shape=(pltpu...]
where the time goes in v5:
time: 44.5 us; the launch traced here: 44.3 us
  Pallas kernels  43.7 us (98%)
  between operations  0.64 us (1%)
    pallas_call x1, Pallas kernels, per_device(): pl.pallas_call(functools.partial(kernel, nr, nc, names), out_shape=(pltpu...  42.5 us
    pallas_call x1, Pallas kernels, per_device(): pl.pallas_call(finish, out_shape=(jax.ShapeDtypeStruct((D, H, W), BF16),...  1.22 us

profile of v5, /device:TPU:1, one launch (start us, length us, event | category | flops | bytes accessed | tf_op | source)
XLA Modules:
  0.0 44.3 jit_solution(5638248887811384958)
XLA Ops:
  0.6 42.5 %shard_map.85 = (bf16[256,8,128]{2,1,0:T(8,128)(2,1)S(1)}, bf16[2,512,256]{2,1,0:T(8,128)(2,1)S(1)}) custom-call(bf16[256,8,128]{2,1,0:T(8,128)(2,1)} %refs_0_.1, f32[1,256]{1,0:T(1,128)} %bitcast.1, bf16[768,256]{1,0:T(8,128)(2,1)} %refs_2_.1, bf16[256,256]{1,0:T(8,128)(2,1)} %refs_3_.1, f32[4]{0:T(128)} %refs_4_.1, bf16[256,8,128]{2,1,0:T(8,128)(2,1)} %refs_5_.1), custom_call_target="tpu_custom_call" | custom-call | tf_op jit(solution)/shard_map/pallas_call | solution.py:543
  43.1 1.2 %shard_map.86 = (bf16[256,8,128]{2,1,0:T(8,128)(2,1)}, f32[768,256]{1,0:T(8,128)}, f32[256,256]{1,0:T(8,128)}) custom-call(bf16[256,8,128]{2,1,0:T(8,128)(2,1)S(1)} %get-tuple-element.5.gl, bf16[2,512,256]{2,1,0:T(8,128)(2,1)S(1)} %get-tuple-element.6.gw), custom_call_target="tpu_custom_call" | custom-call | tf_op jit(solution)/shard_map/pallas_call | solution.py:558

commit v6 on v5

--- a/solution.py
+++ b/solution.py
@@ -56,7 +56,7 @@
 
 
 def at(i, size):
-    return pl.ds(pl.multiple_of(i * size, size), size)
+    return slice(i * size, (i + 1) * size) if isinstance(i, int) else pl.ds(pl.multiple_of(i * size, size), size)
 
 
 def norm_back(raw, inv, grad):
@@ -209,7 +209,7 @@
     edge = {-1: slice(0, near), 1: slice(H * W - near, H * W)}
     part = {-1: slice(0, 32), 1: slice(32, 64)}
     halo = []
-    for i, (dr, dc) in enumerate(DIRS):
+    for i, (dr, dc) in reversed([*enumerate(DIRS)]):
         if dc == 0:
             src, dst = S.xr.at[edge[dr]], S.rx_row.at[i]
         elif dr == 0:
@@ -339,7 +339,7 @@
             first.append((dot(keys, S.qm[j, p]), dot(vals, S.gm[j, p])))
         for t in range(2):
             j = 2 * n + t
-            which = jnp.where(j == 0, 0, jnp.where(j == NB - 1, 2, 1))
+            which = 0 if j == 0 else 2 if j == NB - 1 else 1
             score, prod = first[t]
             tot = jnp.zeros((8, 2 * QC), F32)
             ed = jnp.zeros((8, 2 * QC), F32)
@@ -430,15 +430,18 @@
             c.wait_recv()
 
     begin()
-    lax.fori_loop(0, NB // 2, functools.partial(attention, 0), 0)
+    for n in range(NB // 2):
+        attention(0, n, 0)
     weights(0)
     core0 = to_core(0)
 
     begin()
-    lax.fori_loop(0, NB // 4, functools.partial(attention, 1), 0)
+    for n in range(NB // 4):
+        attention(1, n, 0)
     arrived(core0)
     to_row(0)
-    lax.fori_loop(NB // 4, NB // 2, functools.partial(attention, 1), 0)
+    for n in range(NB // 4, NB // 2):
+        attention(1, n, 0)
     weights(1)
     core1 = to_core(1)
 
@@ -458,7 +461,7 @@
     rows_at = {-1: slice(ABOVE, BELOW), 1: slice(BELOW, UNUSED)}
     cols_at = {-1: slice(0, 8), 1: slice(high, high + 8)}
     back = []
-    for i, (dr, dc) in enumerate(DIRS):
+    for i, (dr, dc) in reversed([*enumerate(DIRS)]):
         if dc == 0:
             S.tx_row[i] = S.gn[rows_at[dr], low:high, :].reshape(RADIUS * W, D).astype(BF16)
             src, dst = S.tx_row.at[i], S.ry_row.at[i]

time: 44.5 us -> 42.7 us (0.960)
  Pallas kernels: 43.7 us -> 42 us
    pallas_call x1, Pallas kernels: 42.5 us -> 40.7 us  [per_device(): pl.pallas_call(functools.partial(kernel, nr, nc, names), out_shape=(pltpu...]
where the time goes in v6:
time: 42.7 us; the launch traced here: 42.6 us
  Pallas kernels  42 us (98%)
  between operations  0.64 us (1%)
    pallas_call x1, Pallas kernels, per_device(): pl.pallas_call(functools.partial(kernel, nr, nc, names), out_shape=(pltpu...  40.7 us
    pallas_call x1, Pallas kernels, per_device(): pl.pallas_call(finish, out_shape=(jax.ShapeDtypeStruct((D, H, W), BF16),...  1.22 us

profile of v6, /device:TPU:1, one launch (start us, length us, event | category | flops | bytes accessed | tf_op | source)
XLA Modules:
  0.0 42.6 jit_solution(3413143609866352066)
XLA Ops:
  0.6 40.7 %shard_map.85 = (bf16[256,8,128]{2,1,0:T(8,128)(2,1)S(1)}, bf16[2,512,256]{2,1,0:T(8,128)(2,1)S(1)}) custom-call(bf16[256,8,128]{2,1,0:T(8,128)(2,1)} %refs_0_.1, f32[1,256]{1,0:T(1,128)} %bitcast.1, bf16[768,256]{1,0:T(8,128)(2,1)} %refs_2_.1, bf16[256,256]{1,0:T(8,128)(2,1)} %refs_3_.1, f32[4]{0:T(128)} %refs_4_.1, bf16[256,8,128]{2,1,0:T(8,128)(2,1)} %refs_5_.1), custom_call_target="tpu_custom_call" | custom-call | tf_op jit(solution)/shard_map/pallas_call | solution.py:546
  41.4 1.2 %shard_map.86 = (bf16[256,8,128]{2,1,0:T(8,128)(2,1)}, f32[768,256]{1,0:T(8,128)}, f32[256,256]{1,0:T(8,128)}) custom-call(bf16[256,8,128]{2,1,0:T(8,128)(2,1)S(1)} %get-tuple-element.5.gl, bf16[2,512,256]{2,1,0:T(8,128)(2,1)S(1)} %get-tuple-element.6.gw), custom_call_target="tpu_custom_call" | custom-call | tf_op jit(solution)/shard_map/pallas_call | solution.py:561

commit v7 on v6

--- a/solution.py
+++ b/solution.py
@@ -27,6 +27,7 @@
 NG = NB + 1
 ER = 16
 ABOVE, BELOW, UNUSED = H, H + RADIUS, H + 2 * RADIUS
+FIRST = 80
 GC = ER * B
 CHUNK = 64
 WP = 4 * PW
@@ -77,10 +78,10 @@
         l32=pltpu.VMEM((D * H, W), F32),
         g32=pltpu.VMEM((D * H, W), F32),
         inv=pltpu.VMEM((H, W), F32),
-        xr=pltpu.VMEM((H * W, D), BF16),
+        xr=pltpu.VMEM((H, W, D), BF16),
         xe32=pltpu.VMEM((2, H * 8, D), F32),
         xe=pltpu.VMEM((2, H * 8, D), BF16),
-        rx_row=pltpu.VMEM((2, RADIUS * W, D), BF16),
+        rx_row=pltpu.VMEM((2, RADIUS, W, D), BF16),
         rx_col=pltpu.VMEM((2, H * 8, D), BF16),
         rx_cor=pltpu.VMEM((4, 32, D), BF16),
         xg=pltpu.VMEM((NG * GC, D), BF16),
@@ -100,8 +101,8 @@
         qm=pltpu.VMEM((NB, 2, PW, 2 * QC), BF16),
         gm=pltpu.VMEM((NB, 2, PW, 2 * QC), BF16),
         mask=pltpu.VMEM((3, 2 * GC, QC), F32),
-        eb=pltpu.VMEM((2, 2 * GC, 2 * QC), BF16),
-        sb=pltpu.VMEM((2, 2 * GC, 2 * QC), BF16),
+        eb=pltpu.VMEM((NB, 2 * GC, 2 * QC), BF16),
+        sb=pltpu.VMEM((NB, 2 * GC, 2 * QC), BF16),
         gk=pltpu.VMEM((PW, GC), F32),
         gv=pltpu.VMEM((PW, GC), F32),
         att=pltpu.VMEM((2, PW, NB * QC), BF16),
@@ -123,8 +124,8 @@
         ys=pltpu.VMEM((2, ny, cc, D), F32),
         cos=pltpu.SMEM((HEADS,), F32),
         s_in=dma((6,)),
-        s_hal=dma((8,)),
-        r_hal=dma((8,)),
+        s_hal=dma((10,)),
+        r_hal=dma((10,)),
         s_ret=dma((8,)),
         r_ret=dma((8,)),
         s_core=dma((2, 2)),
@@ -186,7 +187,7 @@
         return acc + jnp.sum(x * x, axis=0)
 
     loads[0].wait()
-    total = lax.fori_loop(0, D // step, load, jnp.zeros((H, W), F32))
+    total = lax.fori_loop(0, D // step, load, jnp.zeros((H, W), F32), unroll=True)
     S.inv[...] = lax.rsqrt(total * (1.0 / D) + EPS)
     loads[1].wait()
     gain = S.gain[...]
@@ -195,7 +196,7 @@
         x = S.l32[pl.ds(r, D, stride=H), :] * S.inv[r : r + 1, :]
         xn = x.T * gain
         xnb = xn.astype(BF16)
-        S.xr[span(r, W), :] = xnb
+        S.xr[r] = xnb
         S.xe32[0, span(r, 8), :] = xn[:8]
         S.xe32[1, span(r, 8), :] = xn[W - 8 :]
         for j in range(NB):
@@ -205,18 +206,24 @@
     S.xe[...] = S.xe32[...].astype(BF16)
 
     pl.semaphore_wait(barrier, len(partners))
-    near = RADIUS * W
-    edge = {-1: slice(0, near), 1: slice(H * W - near, H * W)}
+    near = {-1: slice(0, RADIUS), 1: slice(H - RADIUS, H)}
     part = {-1: slice(0, 32), 1: slice(32, 64)}
-    halo = []
+    early, late = [], []
     for i, (dr, dc) in reversed([*enumerate(DIRS)]):
         if dc == 0:
-            src, dst = S.xr.at[edge[dr]], S.rx_row.at[i]
-        elif dr == 0:
+            continue
+        if dr == 0:
             src, dst = S.xe.at[(dc + 1) // 2], S.rx_col.at[i - 2]
         else:
             src, dst = S.xe.at[(dc + 1) // 2, part[dr]], S.rx_cor.at[i - 4]
-        halo.append(send(src, dst, S.s_hal.at[i], S.r_hal.at[i], there(dr, dc)))
+        copy = send(src, dst, S.s_hal.at[i], S.r_hal.at[i], there(dr, dc))
+        (early if dc == 1 else late).append(copy)
+    for n, cols in enumerate((slice(0, FIRST), slice(FIRST, W))):
+        for i in range(2):
+            dr = DIRS[i][0]
+            s = 8 * n + i
+            src, dst = S.xr.at[near[dr], cols], S.rx_row.at[i, :, cols]
+            (late if n else early).append(send(src, dst, S.s_hal.at[s], S.r_hal.at[s], there(dr, 0)))
 
     for c in loads[2:]:
         c.wait()
@@ -232,7 +239,7 @@
         S.g32[at(i, step * H), :] = x.reshape(step * H, W)
         return carry
 
-    lax.fori_loop(0, D // step, widen, 0)
+    lax.fori_loop(0, D // step, widen, 0, unroll=True)
     for r in range(H):
         g = S.g32[pl.ds(r, D, stride=H), :].T.astype(BF16)
         for j in range(NB):
@@ -288,32 +295,47 @@
     for g in range(1, NB - 1, 2):
         pairs((g, 0), (g + 1, 0))
 
-    for c in halo:
-        c.wait_recv()
-    left = S.rx_col[1].astype(F32)
-    right = S.rx_col[0].astype(F32)
-
-    def ends(er, first, last, l8, r8):
-        S.xg[span(er, B), :] = jnp.concatenate([l8, first], axis=0).astype(BF16)
-        S.xg[span(NB * ER + er, B), :] = jnp.concatenate([last, r8], axis=0).astype(BF16)
-
-    for r in range(H):
-        ends(r, S.xe32[0, span(r, 8), :], S.xe32[1, span(r, 8), :], left[span(r, 8)], right[span(r, 8)])
-    for down in (0, 1):
-        l_cor = S.rx_cor[2 * down + 1].astype(F32)
-        r_cor = S.rx_cor[2 * down].astype(F32)
-        for i in range(RADIUS):
-            er = (ABOVE if down else BELOW) + i
-            n = i + 1 if down else i
-            line = S.rx_row[down, span(i, W), :].astype(F32)
-            for g in range(1, NB):
-                S.xg[span(g * ER + er, B), :] = line[g * B - 8 : g * B + 8].astype(BF16)
-            ends(er, line[:8], line[-8:], l_cor[span(n, 8)], r_cor[span(n, 8)])
-    for g in range(NG):
-        S.xg[g * GC + UNUSED * B : (g + 1) * GC, :] = jnp.zeros((2 * B, D), BF16)
-    units = [(NB - 1, 0), (0, 0), (NB, 0)] + [(g, 1) for g in range(NG)]
-    for n in range(0, len(units), 2):
-        pairs(*units[n : n + 2])
+    def assemble(copies, groups):
+        for c in copies:
+            c.wait_recv()
+        begin = 0 if groups[0] == 0 else FIRST - B
+        size = FIRST if groups[0] == 0 else W - begin
+        side = 1 if groups[0] == 0 else 0
+        beside = S.rx_col[side].astype(F32)
+        own = S.xe32[1 - side]
+
+        def joined(at_side, inner):
+            return jnp.concatenate([at_side, inner] if side else [inner, at_side], axis=0).astype(BF16)
+
+        for g in groups:
+            S.xg[g * GC + UNUSED * B : (g + 1) * GC, :] = jnp.zeros((2 * B, D), BF16)
+        outer = 0 if side else NB
+        for r in range(H):
+            S.xg[span(outer * ER + r, B), :] = joined(beside[span(r, 8)], own[span(r, 8)])
+        for down in (0, 1):
+            corner = S.rx_cor[2 * down + side].astype(F32)
+            for i in range(RADIUS):
+                er = (ABOVE if down else BELOW) + i
+                line = S.rx_row[down, i, begin : begin + size, :].astype(F32)
+                for g in groups:
+                    a = g * B - 8 - begin
+                    if g != outer:
+                        S.xg[span(g * ER + er, B), :] = line[a : a + B].astype(BF16)
+                inner = line[:8] if side else line[-8:]
+                S.xg[span(outer * ER + er, B), :] = joined(corner[span(i + 1 if down else i, 8)], inner)
+
+    def first_groups():
+        assemble(early, range(0, 5))
+        pairs((0, 0), (0, 1))
+        pairs((1, 1), (2, 1))
+
+    def last_groups():
+        assemble(late, range(5, NG))
+        pairs((5, 1), (6, 1))
+
+    def end_groups():
+        pairs((7, 0), (7, 1))
+        pairs((8, 0), (8, 1))
 
     factor = [S.cos[h] * (1.0 / HW) for h in range(HEADS)]
 
@@ -327,57 +349,66 @@
         S.gkv[p, 0:PW, at(g, GC)] = flat(gk).astype(BF16)
         S.gkv[p, PW : 2 * PW, at(g, GC)] = gv.astype(BF16)
 
-    def attention(p, n, carry):
+    def scores(p, j):
+        o = span(p, PW)
+        keys = jnp.concatenate([S.kc[j, :, o], S.kc[j + 1, :, o]], axis=0)
+        vals = jnp.concatenate([S.vc[j, :, o], S.vc[j + 1, :, o]], axis=0)
+        return dot(keys, S.qm[j, p]), dot(vals, S.gm[j, p])
+
+    def softmax(p, j, score, prod):
+        lgr = by_lane(factor[2 * p : 2 * p + 2]) * math.log2(math.e)
+        which = 0 if j == 0 else 2 if j == NB - 1 else 1
+        tot = jnp.zeros((8, 2 * QC), F32)
+        ed = jnp.zeros((8, 2 * QC), F32)
+        for c in range(0, 2 * GC, CHUNK):
+            mk = S.mask[which, c : c + CHUNK, :]
+            e = jnp.exp2(score[c : c + CHUNK] * lgr) * jnp.concatenate([mk, mk], axis=1)
+            tot = tot + jnp.sum(e.reshape(CHUNK // 8, 8, 2 * QC), axis=0)
+            ed = ed + jnp.sum((e * prod[c : c + CHUNK]).reshape(CHUNK // 8, 8, 2 * QC), axis=0)
+            S.eb[j, c : c + CHUNK, :] = e.astype(BF16)
+        rt = 1.0 / jnp.sum(tot, axis=0, keepdims=True)
+        mean = jnp.sum(ed, axis=0, keepdims=True) * rt
+        for c in range(0, 2 * GC, CHUNK):
+            e = S.eb[j, c : c + CHUNK, :].astype(F32)
+            S.sb[j, c : c + CHUNK, :] = (e * (prod[c : c + CHUNK] - mean)).astype(BF16)
+        return rt
+
+    def backward(p, j, rt, gk, gv):
         o = span(p, PW)
         far = by_lane(factor[2 * p : 2 * p + 2])
-        lgr = far * math.log2(math.e)
-        first = []
-        for t in range(2):
-            j = 2 * n + t
-            keys = jnp.concatenate([S.kc[j, :, o], S.kc[j + 1, :, o]], axis=0)
-            vals = jnp.concatenate([S.vc[j, :, o], S.vc[j + 1, :, o]], axis=0)
-            first.append((dot(keys, S.qm[j, p]), dot(vals, S.gm[j, p])))
-        for t in range(2):
-            j = 2 * n + t
-            which = 0 if j == 0 else 2 if j == NB - 1 else 1
-            score, prod = first[t]
-            tot = jnp.zeros((8, 2 * QC), F32)
-            ed = jnp.zeros((8, 2 * QC), F32)
-            for c in range(0, 2 * GC, CHUNK):
-                mk = S.mask[which, c : c + CHUNK, :]
-                e = jnp.exp2(score[c : c + CHUNK] * lgr) * jnp.concatenate([mk, mk], axis=1)
-                tot = tot + jnp.sum(e.reshape(CHUNK // 8, 8, 2 * QC), axis=0)
-                ed = ed + jnp.sum((e * prod[c : c + CHUNK]).reshape(CHUNK // 8, 8, 2 * QC), axis=0)
-                S.eb[t, c : c + CHUNK, :] = e.astype(BF16)
-            rt = 1.0 / jnp.sum(tot, axis=0, keepdims=True)
-            mean = jnp.sum(ed, axis=0, keepdims=True) * rt
-            for c in range(0, 2 * GC, CHUNK):
-                e = S.eb[t, c : c + CHUNK, :].astype(F32)
-                S.sb[t, c : c + CHUNK, :] = (e * (prod[c : c + CHUNK] - mean)).astype(BF16)
-            prob = S.eb[t]
-            slope = S.sb[t]
-            keys_t = jnp.concatenate([S.kt[j, o, :], S.kt[j + 1, o, :]], axis=1)
-            vals_t = jnp.concatenate([S.vt[j, o, :], S.vt[j + 1, o, :]], axis=1)
-            attn = dot(vals_t, prob) * rt
-            grad_q = dot(keys_t, slope) * (rt * far)
-            for i in range(2):
-                c, lanes = span(i, HW), span(i, QC)
-                S.att[p, c, at(j, QC)] = attn[c, lanes].astype(BF16)
-                raw = S.qraw[j, span(2 * p + i, HW), :]
-                g = norm_back(heads(raw), S.qinv[j, 2 * p + i : 2 * p + i + 1], heads(grad_q[c, lanes]))
-                S.gqb[p, c, at(j, QC)] = flat(g).astype(BF16)
-            qs = (S.qm[j, p].astype(F32) * rt).astype(BF16)
-            gs = (S.gm[j, p].astype(F32) * rt).astype(BF16)
-            grad_k = dot_nt(qs, slope)
-            grad_v = dot_nt(gs, prob)
-            key_done(p, j, S.gk[...] + grad_k[:, :GC], S.gv[...] + grad_v[:, :GC])
-            S.gk[...] = grad_k[:, GC:]
-            S.gv[...] = grad_v[:, GC:]
-        return carry
-
-    def begin():
-        S.gk[...] = jnp.zeros((PW, GC), F32)
-        S.gv[...] = jnp.zeros((PW, GC), F32)
+        prob = S.eb[j]
+        slope = S.sb[j]
+        keys_t = jnp.concatenate([S.kt[j, o, :], S.kt[j + 1, o, :]], axis=1)
+        vals_t = jnp.concatenate([S.vt[j, o, :], S.vt[j + 1, o, :]], axis=1)
+        attn = dot(vals_t, prob) * rt
+        grad_q = dot(keys_t, slope) * (rt * far)
+        for i in range(2):
+            c, lanes = span(i, HW), span(i, QC)
+            S.att[p, c, at(j, QC)] = attn[c, lanes].astype(BF16)
+            raw = S.qraw[j, span(2 * p + i, HW), :]
+            g = norm_back(heads(raw), S.qinv[j, 2 * p + i : 2 * p + i + 1], heads(grad_q[c, lanes]))
+            S.gqb[p, c, at(j, QC)] = flat(g).astype(BF16)
+        qs = (S.qm[j, p].astype(F32) * rt).astype(BF16)
+        gs = (S.gm[j, p].astype(F32) * rt).astype(BF16)
+        grad_k = dot_nt(qs, slope)
+        grad_v = dot_nt(gs, prob)
+        key_done(p, j, gk + grad_k[:, :GC], gv + grad_v[:, :GC])
+        return grad_k[:, GC:], grad_v[:, GC:]
+
+    def attention(p, ahead):
+        gk, gv = jnp.zeros((PW, GC), F32), jnp.zeros((PW, GC), F32)
+        first, rts = {}, {}
+        for j in range(NB + 1):
+            if j in ahead:
+                ahead[j]()
+            if j < NB:
+                first[j] = scores(p, j)
+            if j < NB:
+                rts[j] = softmax(p, j, *first.pop(j))
+            if 0 <= j - 1 < NB:
+                gk, gv = backward(p, j - 1, rts.pop(j - 1), gk, gv)
+        S.gk[...] = gk
+        S.gv[...] = gv
 
     def weights(p):
         key_done(p, NB, S.gk[...], S.gv[...])
@@ -429,19 +460,15 @@
         for c in copies:
             c.wait_recv()
 
-    begin()
-    for n in range(NB // 2):
-        attention(0, n, 0)
+    attention(0, {0: first_groups, 2: lambda: pairs((3, 1), (4, 1)), 4: last_groups, 6: end_groups})
     weights(0)
     core0 = to_core(0)
 
-    begin()
-    for n in range(NB // 4):
-        attention(1, n, 0)
-    arrived(core0)
-    to_row(0)
-    for n in range(NB // 4, NB // 2):
-        attention(1, n, 0)
+    def midway():
+        arrived(core0)
+        to_row(0)
+
+    attention(1, {NB // 2: midway})
     weights(1)
     core1 = to_core(1)
 
@@ -511,7 +538,7 @@
         S.gl[pl.ds(i * step, step)] = S.l32[at(i, step * H), :].reshape(step, H, W).astype(BF16)
         return carry
 
-    lax.fori_loop(0, D // step, store, 0)
+    lax.fori_loop(0, D // step, store, 0, unroll=True)
 
     departed()
     whole_row(0, S.s_pl.at[0, 0])

time: 42.7 us -> 42 us (0.984)
  Pallas kernels: 42 us -> 41.2 us
    pallas_call x1, Pallas kernels: 40.7 us -> 40 us  [per_device(): pl.pallas_call(functools.partial(kernel, nr, nc, names), out_shape=(pltpu...]
where the time goes in v7:
time: 42 us; the launch traced here: 41.9 us
  Pallas kernels  41.2 us (98%)
  between operations  0.64 us (2%)
    pallas_call x1, Pallas kernels, per_device(): pl.pallas_call(functools.partial(kernel, nr, nc, names), out_shape=(pltpu...  40 us
    pallas_call x1, Pallas kernels, per_device(): pl.pallas_call(finish, out_shape=(jax.ShapeDtypeStruct((D, H, W), BF16),...  1.22 us

profile of v7, /device:TPU:1, one launch (start us, length us, event | category | flops | bytes accessed | tf_op | source)
XLA Modules:
  0.0 41.9 jit_solution(5690513126656273101)
XLA Ops:
  0.6 40.0 %shard_map.85 = (bf16[256,8,128]{2,1,0:T(8,128)(2,1)S(1)}, bf16[2,512,256]{2,1,0:T(8,128)(2,1)S(1)}) custom-call(bf16[256,8,128]{2,1,0:T(8,128)(2,1)} %refs_0_.1, f32[1,256]{1,0:T(1,128)} %bitcast.1, bf16[768,256]{1,0:T(8,128)(2,1)} %refs_2_.1, bf16[256,256]{1,0:T(8,128)(2,1)} %refs_3_.1, f32[4]{0:T(128)} %refs_4_.1, bf16[256,8,128]{2,1,0:T(8,128)(2,1)} %refs_5_.1), custom_call_target="tpu_custom_call" | custom-call | tf_op jit(solution)/shard_map/pallas_call | solution.py:573
  40.7 1.2 %shard_map.86 = (bf16[256,8,128]{2,1,0:T(8,128)(2,1)}, f32[768,256]{1,0:T(8,128)}, f32[256,256]{1,0:T(8,128)}) custom-call(bf16[256,8,128]{2,1,0:T(8,128)(2,1)S(1)} %get-tuple-element.5.gl, bf16[2,512,256]{2,1,0:T(8,128)(2,1)S(1)} %get-tuple-element.6.gw), custom_call_target="tpu_custom_call" | custom-call | tf_op jit(solution)/shard_map/pallas_call | solution.py:588

commit v8 on v7

--- a/solution.py
+++ b/solution.py
@@ -373,7 +373,7 @@
             S.sb[j, c : c + CHUNK, :] = (e * (prod[c : c + CHUNK] - mean)).astype(BF16)
         return rt
 
-    def backward(p, j, rt, gk, gv):
+    def backward(p, j, rt):
         o = span(p, PW)
         far = by_lane(factor[2 * p : 2 * p + 2])
         prob = S.eb[j]
@@ -388,6 +388,10 @@
             raw = S.qraw[j, span(2 * p + i, HW), :]
             g = norm_back(heads(raw), S.qinv[j, 2 * p + i : 2 * p + i + 1], heads(grad_q[c, lanes]))
             S.gqb[p, c, at(j, QC)] = flat(g).astype(BF16)
+
+    def backward_keys(p, j, rt, gk, gv):
+        prob = S.eb[j]
+        slope = S.sb[j]
         qs = (S.qm[j, p].astype(F32) * rt).astype(BF16)
         gs = (S.gm[j, p].astype(F32) * rt).astype(BF16)
         grad_k = dot_nt(qs, slope)
@@ -406,7 +410,8 @@
             if j < NB:
                 rts[j] = softmax(p, j, *first.pop(j))
             if 0 <= j - 1 < NB:
-                gk, gv = backward(p, j - 1, rts.pop(j - 1), gk, gv)
+                gk, gv = backward_keys(p, j - 1, rts[j - 1], gk, gv)
+                backward(p, j - 1, rts.pop(j - 1))
         S.gk[...] = gk
         S.gv[...] = gv
 

time: 42 us -> 41.8 us (level)
  no operation moved by 1% of the time
where the time goes in v8:
time: 41.8 us; the launch traced here: 41.7 us
  Pallas kernels  41 us (98%)
  between operations  0.64 us (2%)
    pallas_call x1, Pallas kernels, per_device(): pl.pallas_call(functools.partial(kernel, nr, nc, names), out_shape=(pltpu...  39.8 us
    pallas_call x1, Pallas kernels, per_device(): pl.pallas_call(finish, out_shape=(jax.ShapeDtypeStruct((D, H, W), BF16),...  1.22 us

profile of v8, /device:TPU:1, one launch (start us, length us, event | category | flops | bytes accessed | tf_op | source)
XLA Modules:
  0.0 41.7 jit_solution(16315042649299872784)
XLA Ops:
  0.6 39.8 %shard_map.85 = (bf16[256,8,128]{2,1,0:T(8,128)(2,1)S(1)}, bf16[2,512,256]{2,1,0:T(8,128)(2,1)S(1)}) custom-call(bf16[256,8,128]{2,1,0:T(8,128)(2,1)} %refs_0_.1, f32[1,256]{1,0:T(1,128)} %bitcast.1, bf16[768,256]{1,0:T(8,128)(2,1)} %refs_2_.1, bf16[256,256]{1,0:T(8,128)(2,1)} %refs_3_.1, f32[4]{0:T(128)} %refs_4_.1, bf16[256,8,128]{2,1,0:T(8,128)(2,1)} %refs_5_.1), custom_call_target="tpu_custom_call" | custom-call | tf_op jit(solution)/shard_map/pallas_call | solution.py:578
  40.5 1.2 %shard_map.86 = (bf16[256,8,128]{2,1,0:T(8,128)(2,1)}, f32[768,256]{1,0:T(8,128)}, f32[256,256]{1,0:T(8,128)}) custom-call(bf16[256,8,128]{2,1,0:T(8,128)(2,1)S(1)} %get-tuple-element.5.gl, bf16[2,512,256]{2,1,0:T(8,128)(2,1)S(1)} %get-tuple-element.6.gw), custom_call_target="tpu_custom_call" | custom-call | tf_op jit(solution)/shard_map/pallas_call | solution.py:593
